TPU v7x, 32 devices: a whole 2x2x4 slice. The times are simulated.
32 devices in a mesh: row: 4 (over y, x), col: 8 (over z, core).
Axes of the slice: x: 2, y: 2, z: 4, core: 2. Of those that a mesh axis runs over, the one named last changes fastest.
Arguments:
- features: bfloat16 [64, 512, 512], P(None, 'col', 'row'), may hold values from -120 to 120
- conv_first: bfloat16 [9, 64, 64], replicated, may hold values from -0.25 to 0.25
- conv_second: bfloat16 [9, 64, 64], replicated, may hold values from -0.25 to 0.25
- head_weight: bfloat16 [37, 64], replicated, may hold values from -0.75 to 0.75
- head_bias: float32 [37], replicated, may hold values from -4 to 4
- cotangent: bfloat16 [37, 512, 512], P(None, 'col', 'row'), may hold values from -6 to 6
Outputs:
- logits: bfloat16 [37, 512, 512], P(None, 'col', 'row')
- input_grad: bfloat16 [64, 512, 512], P(None, 'col', 'row')
- grad_first: float32 [9, 64, 64], replicated
- grad_second: float32 [9, 64, 64], replicated
- grad_head: float32 [37, 64], replicated
- grad_bias: float32 [37], replicated
All inputs are finite; a program needn't handle non-finite values.
Results may differ from a plain program's by a relative error of at most 0.007.
Values may be sent and summed in bfloat16 or wider, within the bound.
A program may use at most 128 MiB of HBM per device.

v0:
```python
import functools

import jax
import jax.numpy as jnp
from jax import lax
from jax.experimental import pallas as pl
from jax.experimental.pallas import tpu as pltpu
from jax.sharding import PartitionSpec as P

DILATION_STEP = 16


epsilon = 1e-05


def elu_apply(value_entries):
    return jnp.where(
        value_entries > 0, value_entries, jnp.exp(jnp.minimum(value_entries, 0.0)) - 1.0
    )


def elu_slope(value_entries):
    return jnp.where(value_entries > 0, 1.0, jnp.exp(jnp.minimum(value_entries, 0.0)))


def greet(axis, count):
    me = lax.axis_index(axis)
    barrier = pltpu.get_barrier_semaphore()
    for step in range(1, count):
        pl.semaphore_signal(
            barrier,
            inc=1,
            device_id={axis: lax.rem(me + step, count)},
            device_id_type=pl.DeviceIdType.MESH,
        )


def share(axis, count, source, landing, send_sem, recv_sem):
    me = lax.axis_index(axis)
    copies = []
    for step in range(1, count):
        target = lax.rem(me + step, count)
        copy = pltpu.make_async_remote_copy(
            src_ref=source(target),
            dst_ref=landing.at[me],
            send_sem=send_sem.at[step - 1],
            recv_sem=recv_sem.at[step - 1],
            device_id={axis: target},
            device_id_type=pl.DeviceIdType.MESH,
        )
        copy.start()
        copies.append(copy)
    return copies


def finish(copies):
    for copy in copies:
        copy.wait()


def in_order(ref, count):
    total = ref[0]
    for index in range(1, count):
        total = total + ref[index]
    return total


def mirror(tensor):
    rows, cols = lax.axis_size("row"), lax.axis_size("col")
    ratio = cols // rows
    edge = tensor.shape[1]
    col = lax.axis_index("col")
    halves = tensor.reshape(tensor.shape[0], edge, ratio, edge).transpose(2, 0, 3, 1)
    arrived = []
    for step in range(ratio):
        pairs = [
            (r * cols + c, (c // ratio) * cols + ratio * r + (c + step) % ratio)
            for r in range(rows)
            for c in range(cols)
        ]
        mine = lax.dynamic_index_in_dim(halves, lax.rem(col + step, ratio), 0, False)
        arrived.append(lax.ppermute(mine, ("row", "col"), pairs))
    stacked = jnp.stack(arrived)
    places = lax.rem(col - jnp.arange(ratio) + ratio * cols, ratio)
    ordered = [
        lax.dynamic_index_in_dim(stacked, places[index], 0, False) for index in range(ratio)
    ]
    return jnp.concatenate(ordered, axis=2)


def dma(count):
    return pltpu.SemaphoreType.DMA((count,))


DIRECTIONS = ((0, -1), (0, 1), (-1, 0), (1, 0), (-1, -1), (-1, 1), (1, -1), (1, 1))


def meet(rows, cols):
    row, col = lax.axis_index("row"), lax.axis_index("col")
    greet("row", rows)
    greet("col", cols)
    barrier = pltpu.get_barrier_semaphore()
    corners = [pair for pair in DIRECTIONS if pair[0] and pair[1]]
    for down, across in corners:
        pl.semaphore_signal(
            barrier,
            inc=1,
            device_id={
                "row": lax.rem(row + rows + down, rows),
                "col": lax.rem(col + cols + across, cols),
            },
            device_id_type=pl.DeviceIdType.MESH,
        )
    pl.semaphore_wait(barrier, rows + cols - 2 + len(corners))


class Plan:
    def __init__(self, channels, height, lanes, rows, cols):
        self.channels, self.height, self.lanes = channels, height, lanes
        self.rows, self.cols = rows, cols
        self.margin = DILATION_STEP * lanes
        self.cells = height * lanes
        self.group = lanes // DILATION_STEP
        self.chunk = self.group * lanes
        self.chunks = self.cells // self.chunk
        self.width = self.cells + 2 * self.margin
        self.edge = DILATION_STEP // self.group * lanes
        self.strip = self.chunks * lanes
        self.strip_width = self.strip + 2 * self.edge

    def wide_scratch(self):
        return [
            pltpu.VMEM((self.channels, self.strip), jnp.bfloat16),
            pltpu.VMEM((self.channels, self.strip), jnp.bfloat16),
            pltpu.VMEM((self.channels, self.strip_width), jnp.bfloat16),
            pltpu.VMEM((self.channels, self.strip_width), jnp.bfloat16),
            dma(8),
            dma(8),
        ]

    def sum_scratch(self):
        return [
            pltpu.VMEM((self.rows, 8, 128), jnp.float32),
            pltpu.VMEM((self.cols, 8, 128), jnp.float32),
            dma(self.rows - 1),
            dma(self.rows - 1),
            dma(self.cols - 1),
            dma(self.cols - 1),
        ]

    def at(self, index, offset=0, size=None):
        size = self.chunk if size is None else size
        return pl.ds(pl.multiple_of(index * size + offset, 128), size)


def clear(plan, wide, low, high):
    middle = slice(plan.channels, 2 * plan.channels)
    blank = jnp.zeros((plan.channels, plan.margin), jnp.bfloat16)
    wide[middle, : plan.margin] = blank
    wide[middle, plan.width - plan.margin :] = blank
    low[...] = jnp.zeros_like(low)
    high[...] = jnp.zeros_like(high)


def emit(plan, wide, last, first, index, values):
    n, lanes, step = plan.channels, plan.lanes, DILATION_STEP
    place = plan.at(index, plan.margin)
    lane = lax.broadcasted_iota(jnp.int32, (n, lanes), 1)
    wide[n : 2 * n, place] = values.astype(jnp.bfloat16)
    later, sooner = [], []
    tail, lead = jnp.zeros((n, lanes), jnp.float32), jnp.zeros((n, lanes), jnp.float32)
    for m in range(plan.group):
        line = values[:, m * lanes : (m + 1) * lanes]
        right = pltpu.roll(line, step, 1)
        left = pltpu.roll(line, lanes - step, 1)
        later.append(right.astype(jnp.bfloat16))
        sooner.append(left.astype(jnp.bfloat16))
        mine = (lane >= m * step) & (lane < (m + 1) * step)
        tail = jnp.where(mine, pltpu.roll(right, m * step, 1) if m else right, tail)
        lead = jnp.where(mine, pltpu.roll(line, m * step, 1) if m else line, lead)
    wide[0:n, place] = jnp.concatenate(later, axis=1)
    wide[2 * n : 3 * n, place] = jnp.concatenate(sooner, axis=1)
    spot = plan.at(index, 0, lanes)
    last[:, spot] = tail.astype(jnp.bfloat16)
    first[:, spot] = lead.astype(jnp.bfloat16)


def halo_copies(plan, wide, last, first, low, high, send_sem, recv_sem):
    row, col = lax.axis_index("row"), lax.axis_index("col")
    n = plan.channels
    middle = slice(n, 2 * n)
    found = []
    for index, (down, across) in enumerate(DIRECTIONS):
        if down == 0:
            if across < 0:
                source = wide.at[middle, plan.margin : 2 * plan.margin]
                target = wide.at[middle, plan.width - plan.margin : plan.width]
            else:
                source = wide.at[middle, plan.cells : plan.cells + plan.margin]
                target = wide.at[middle, 0 : plan.margin]
        else:
            strip, landing = (last, low) if down > 0 else (first, high)
            if across == 0:
                source, target = strip, landing.at[:, plan.edge : plan.edge + plan.strip]
            elif across > 0:
                source = strip.at[:, plan.strip - plan.edge : plan.strip]
                target = landing.at[:, 0 : plan.edge]
            else:
                source = strip.at[:, 0 : plan.edge]
                target = landing.at[:, plan.edge + plan.strip : plan.strip_width]
        there = {
            "row": jnp.clip(row + down, 0, plan.rows - 1),
            "col": jnp.clip(col + across, 0, plan.cols - 1),
        }
        copy = pltpu.make_async_remote_copy(
            src_ref=source,
            dst_ref=target,
            send_sem=send_sem.at[index],
            recv_sem=recv_sem.at[index],
            device_id=there,
            device_id_type=pl.DeviceIdType.MESH,
        )

        def inside(r, c):
            return (r >= 0) & (r < plan.rows) & (c >= 0) & (c < plan.cols)

        found.append((copy, inside(row + down, col + across), inside(row - down, col - across)))
    return found


def halo_start(copies):
    for copy, sends, _ in copies:
        pl.when(sends)(copy.start)


def halo_wait(copies):
    for copy, sends, receives in copies:
        pl.when(receives)(copy.wait_recv)
        pl.when(sends)(copy.wait_send)


def mend(plan, wide, low, high):
    n, lanes, step = plan.channels, plan.lanes, DILATION_STEP
    lane = lax.broadcasted_iota(jnp.int32, (n, lanes), 1)

    def fill(index, fresh):
        place = plan.at(index)
        spot = plan.at(index, 0, lanes)
        before = low[:, spot].astype(jnp.float32)
        after = high[:, spot].astype(jnp.float32)
        middle = wide[n : 2 * n, place].astype(jnp.float32) if fresh else None
        old_later = None if fresh else wide[0:n, place].astype(jnp.float32)
        old_sooner = None if fresh else wide[2 * n : 3 * n, place].astype(jnp.float32)
        later, sooner = [], []
        for m in range(plan.group):
            line = slice(m * lanes, (m + 1) * lanes)
            if fresh:
                right = pltpu.roll(middle[:, line], step, 1)
                left = pltpu.roll(middle[:, line], lanes - step, 1)
            else:
                right, left = old_later[:, line], old_sooner[:, line]
            enter = pltpu.roll(before, (lanes - m * step) % lanes, 1) if m else before
            back = (lanes - step - m * step) % lanes
            leave = pltpu.roll(after, back, 1) if back else after
            later.append(jnp.where(lane < step, enter, right).astype(jnp.bfloat16))
            sooner.append(jnp.where(lane >= lanes - step, leave, left).astype(jnp.bfloat16))
        wide[0:n, place] = jnp.concatenate(later, axis=1)
        wide[2 * n : 3 * n, place] = jnp.concatenate(sooner, axis=1)

    side = plan.margin // plan.chunk

    def outer(index, carry):
        fill(index, True)
        fill(index + side + plan.chunks, True)
        return carry

    def inner(index, carry):
        fill(index + side, False)
        return carry

    lax.fori_loop(0, side, outer, 0)
    lax.fori_loop(0, plan.chunks, inner, 0)


def conv_chunk(plan, wide, weight, index):
    total = None
    for b in range(3):
        part = jnp.dot(
            weight[b],
            wide[:, plan.at(index, b * plan.margin)],
            preferred_element_type=jnp.float32,
        )
        total = part if total is None else total + part
    return total


def weight_chunk(plan, wide, gradient, index):
    return [
        lax.dot_general(
            gradient,
            wide[:, plan.at(index, b * plan.margin)],
            (((1,), (1,)), ((), ())),
            preferred_element_type=jnp.float32,
        )
        for b in range(3)
    ]


def total_sums(plan, pair, over_row, over_col, row_out, row_in, col_out, col_in):
    row, col = lax.axis_index("row"), lax.axis_index("col")
    n = plan.channels
    lane = lax.broadcasted_iota(jnp.int32, (n, 128), 1)
    both = jnp.where(lane == 0, pair[0], jnp.where(lane == 1, pair[1], 0.0))
    square = jnp.concatenate([both, jnp.zeros((128 - n, 128), jnp.float32)], axis=0)
    over_row[row] = square.T[0:8]
    finish(share("row", plan.rows, lambda t: over_row.at[row], over_row, row_out, row_in))
    over_col[col] = in_order(over_row, plan.rows)
    finish(share("col", plan.cols, lambda t: over_col.at[col], over_col, col_out, col_in))
    summed = in_order(over_col, plan.cols)
    back = jnp.concatenate([summed, jnp.zeros((120, 128), jnp.float32)], axis=0).T
    return back[0:n, 0:1], back[0:n, 1:2]


def pair_of(first, second):
    return jnp.sum(first, axis=1, keepdims=True), jnp.sum(second, axis=1, keepdims=True)


def forward_kernel(plan, cell_count, *refs):
    x, w_first, w_second, w_head, bias = refs[:5]
    wide_x, wide_h, n_first, n_second, raw, hidden, inv_first, inv_second = refs[5:13]
    act = refs[13]
    ends_x, ends_h = refs[14:20], refs[20:26]
    sums_first, sums_second = refs[26:32], refs[32:38]
    n = plan.channels
    zero = jnp.zeros((n, 1), jnp.float32)
    clear(plan, wide_x, ends_x[2], ends_x[3])
    clear(plan, wide_h, ends_h[2], ends_h[3])
    meet(plan.rows, plan.cols)

    def load(index, carry):
        emit(plan, wide_x, ends_x[0], ends_x[1], index, x[:, plan.at(index)].astype(jnp.float32))
        return carry

    lax.fori_loop(0, plan.chunks, load, 0)
    copies = halo_copies(plan, wide_x, *ends_x)
    halo_start(copies)
    halo_wait(copies)
    mend(plan, wide_x, ends_x[2], ends_x[3])

    def convolve(wide, weight):
        def body(index, carry):
            part = conv_chunk(plan, wide, weight, index)
            act[:, plan.at(index)] = part
            found = pair_of(part, part * part)
            return carry[0] + found[0], carry[1] + found[1]

        return lax.fori_loop(0, plan.chunks, body, (zero, zero))

    def moments(pair, scratch, kept):
        totals, squares = total_sums(plan, pair, *scratch)
        average = totals / cell_count
        inverse = lax.rsqrt(squares / cell_count - average * average + epsilon)
        kept[...] = jnp.broadcast_to(inverse, kept.shape)
        return average, inverse

    average, inverse = moments(convolve(wide_x, w_first), sums_first, inv_first)

    def middle(index, carry):
        normed = (act[:, plan.at(index)] - average) * inverse
        n_first[:, plan.at(index)] = normed
        emit(plan, wide_h, ends_h[0], ends_h[1], index, elu_apply(normed))
        return carry

    lax.fori_loop(0, plan.chunks, middle, 0)
    copies = halo_copies(plan, wide_h, *ends_h)
    halo_start(copies)
    halo_wait(copies)
    mend(plan, wide_h, ends_h[2], ends_h[3])
    average_2, inverse_2 = moments(convolve(wide_h, w_second), sums_second, inv_second)

    def tail(index, carry):
        place = plan.at(index)
        normed = (act[:, place] - average_2) * inverse_2
        n_second[:, place] = normed
        out = elu_apply(normed + x[:, place].astype(jnp.float32)).astype(jnp.bfloat16)
        hidden[:, place] = out
        raw[:, place] = (
            jnp.dot(w_head[...], out, preferred_element_type=jnp.float32) + bias[:, 0:1]
        )
        return carry

    lax.fori_loop(0, plan.chunks, tail, 0)


def backward_kernel(plan, cell_count, depth, *refs):
    (x, wide_x, wide_h, n_first, n_second, inv_first, inv_second) = refs[:7]
    sym, hidden, w_first, w_second, w_head = refs[7:12]
    grad_x, gathered = refs[12:14]
    wide_2, wide_1, slope_grad, inner_grad = refs[14:18]
    ends_2, ends_1 = refs[18:24], refs[24:30]
    sums_2, sums_1 = refs[30:36], refs[36:42]
    (mine, parts, over_row, whole, part_out, part_in) = refs[42:48]
    row_out, row_in, col_out, col_in = refs[48:52]
    row, col = lax.axis_index("row"), lax.axis_index("col")
    n, bins = plan.channels, sym.shape[0]
    zero = jnp.zeros((n, 1), jnp.float32)
    clear(plan, wide_2, ends_2[2], ends_2[3])
    clear(plan, wide_1, ends_1[2], ends_1[3])
    mine[...] = jnp.zeros_like(mine)
    meet(plan.rows, plan.cols)
    head_at = 6 * n

    def start(index, carry):
        place = plan.at(index)
        sym_part = sym[:, place]
        summed = n_second[:, place] + x[:, place].astype(jnp.float32)
        part = jnp.dot(w_head[...], sym_part, preferred_element_type=jnp.float32)
        part = part * elu_slope(summed)
        slope_grad[:, place] = part
        mine[head_at : head_at + bins, 0:n] += lax.dot_general(
            sym_part, hidden[:, place], (((1,), (1,)), ((), ())),
            preferred_element_type=jnp.float32,
        )
        mine[head_at : head_at + bins, 128:256] += jnp.broadcast_to(
            jnp.sum(sym_part.astype(jnp.float32), axis=1, keepdims=True), (bins, 128)
        )
        found = pair_of(part, part * n_second[:, place])
        return carry[0] + found[0], carry[1] + found[1]

    pair = lax.fori_loop(0, plan.chunks, start, (zero, zero))

    def step_back(pair, scratch, source, normed, inverse_ref, wide, ends):
        first_sum, second_sum = total_sums(plan, pair, *scratch)
        first_mean, second_mean = first_sum / cell_count, second_sum / cell_count
        inverse = inverse_ref[:, 0:1]

        def body(index, carry):
            place = plan.at(index)
            value = inverse * (source[:, place] - first_mean - normed[:, place] * second_mean)
            emit(plan, wide, ends[0], ends[1], index, value)
            return carry

        lax.fori_loop(0, plan.chunks, body, 0)
        copies = halo_copies(plan, wide, *ends)
        halo_start(copies)
        return copies

    def weigh(wide, against, base):
        def body(index, carry):
            gradient = wide[n : 2 * n, plan.at(index, plan.margin)]
            for b, part in enumerate(weight_chunk(plan, against, gradient, index)):
                mine[base + b * n : base + (b + 1) * n, 0 : 3 * n] += part
            return carry

        lax.fori_loop(0, plan.chunks, body, 0)

    copies = step_back(pair, sums_2, slope_grad, n_second, inv_second, wide_2, ends_2)
    weigh(wide_2, wide_h, 3 * n)
    halo_wait(copies)
    mend(plan, wide_2, ends_2[2], ends_2[3])

    def through(index, carry):
        place = plan.at(index)
        normed = n_first[:, place]
        part = conv_chunk(plan, wide_2, w_second, index) * elu_slope(normed)
        inner_grad[:, place] = part
        found = pair_of(part, part * normed)
        return carry[0] + found[0], carry[1] + found[1]

    pair = lax.fori_loop(0, plan.chunks, through, (zero, zero))
    copies = step_back(pair, sums_1, inner_grad, n_first, inv_first, wide_1, ends_1)
    weigh(wide_1, wide_x, 0)

    def piece(ref, t):
        return ref.at[pl.ds(pl.multiple_of(t * depth, 8), depth)]

    parts[col] = piece(mine, col)[...]
    sums = share("col", plan.cols, lambda t: piece(mine, t), parts, part_out, part_in)
    halo_wait(copies)
    mend(plan, wide_1, ends_1[2], ends_1[3])
    finish(sums)
    over_row[row] = in_order(parts, plan.cols)
    sums = share("row", plan.rows, lambda t: over_row.at[row], over_row, row_out, row_in)

    def last(index, carry):
        place = plan.at(index)
        part = conv_chunk(plan, wide_1, w_first, index) + slope_grad[:, place]
        grad_x[:, place] = part.astype(jnp.bfloat16)
        return carry

    lax.fori_loop(0, plan.chunks, last, 0)
    finish(sums)
    whole[col] = in_order(over_row, plan.rows)
    finish(share("col", plan.cols, lambda t: whole.at[col], whole, col_out, col_in))
    gathered[...] = whole[...]


def vmem(count):
    return [pl.BlockSpec(memory_space=pltpu.VMEM)] * count


def taps(weights, adjoint):
    count, outs, ins = weights.shape
    grid = weights.reshape(3, 3, outs, ins)
    if adjoint:
        return grid[::-1, ::-1].transpose(1, 3, 0, 2).reshape(3, ins, 3 * outs)
    return grid.transpose(1, 2, 0, 3).reshape(3, outs, 3 * ins)


def on_device(features, conv_first, conv_second, head_weight, head_bias, cotangent):
    channels, height, lanes = features.shape
    rows, cols = lax.axis_size("row"), lax.axis_size("col")
    length = height * cols
    cell_count = float(length * length)
    bins = head_weight.shape[0]
    padded = -(-bins // 16) * 16
    plan = Plan(channels, height, lanes, rows, cols)
    cells, width = plan.cells, plan.width
    cot_mirror = mirror(cotangent)
    grad_sym = (0.5 * (cotangent.astype(jnp.float32) + cot_mirror.astype(jnp.float32))).astype(
        jnp.bfloat16
    )
    sym = jnp.pad(grad_sym.reshape(bins, cells), ((0, padded - bins), (0, 0)))
    x = features.reshape(channels, cells)
    w_head = jnp.pad(head_weight, ((0, padded - bins), (0, 0)))
    bias = jnp.broadcast_to(jnp.pad(head_bias, (0, padded - bins))[:, None], (padded, 128))
    wide_shape = jax.ShapeDtypeStruct((3 * channels, width), jnp.bfloat16)
    full_shape = jax.ShapeDtypeStruct((channels, cells), jnp.float32)
    short_shape = jax.ShapeDtypeStruct((channels, cells), jnp.bfloat16)
    inverse_shape = jax.ShapeDtypeStruct((channels, 128), jnp.float32)
    flops = 2 * 9 * channels * channels * cells
    wide_x, wide_h, n_first, n_second, raw, hidden, inv_first, inv_second = pl.pallas_call(
        functools.partial(forward_kernel, plan, cell_count),
        out_shape=(
            wide_shape,
            wide_shape,
            full_shape,
            full_shape,
            jax.ShapeDtypeStruct((padded, cells), jnp.float32),
            short_shape,
            inverse_shape,
            inverse_shape,
        ),
        in_specs=vmem(5),
        out_specs=tuple(vmem(8)),
        scratch_shapes=[
            pltpu.VMEM((channels, cells), jnp.float32),
            *plan.wide_scratch(),
            *plan.wide_scratch(),
            *plan.sum_scratch(),
            *plan.sum_scratch(),
        ],
        compiler_params=pltpu.CompilerParams(
            collective_id=0, has_side_effects=True, vmem_limit_bytes=40 * 2**20
        ),
        cost_estimate=pl.CostEstimate(
            flops=20 * flops, bytes_accessed=200 * 2**20, transcendentals=0
        ),
    )(x, taps(conv_first, False), taps(conv_second, False), w_head, bias)
    raw_logits = raw[:bins].reshape(bins, height, lanes)
    logit_mirror = mirror(raw_logits.astype(jnp.bfloat16)).astype(jnp.float32)
    logits = (0.5 * (raw_logits + logit_mirror)).astype(jnp.bfloat16)
    total_rows = 6 * channels + padded
    depth = -(-total_rows // (cols * 8)) * 8
    grad_x, gathered = pl.pallas_call(
        functools.partial(backward_kernel, plan, cell_count, depth),
        out_shape=(short_shape, jax.ShapeDtypeStruct((cols, depth, 256), jnp.float32)),
        in_specs=vmem(12),
        out_specs=tuple(vmem(2)),
        scratch_shapes=[
            pltpu.VMEM(wide_shape.shape, jnp.bfloat16),
            pltpu.VMEM(wide_shape.shape, jnp.bfloat16),
            pltpu.VMEM((channels, cells), jnp.float32),
            pltpu.VMEM((channels, cells), jnp.float32),
            *plan.wide_scratch(),
            *plan.wide_scratch(),
            *plan.sum_scratch(),
            *plan.sum_scratch(),
            pltpu.VMEM((cols * depth, 256), jnp.float32),
            pltpu.VMEM((cols, depth, 256), jnp.float32),
            pltpu.VMEM((rows, depth, 256), jnp.float32),
            pltpu.VMEM((cols, depth, 256), jnp.float32),
            dma(cols - 1),
            dma(cols - 1),
            dma(rows - 1),
            dma(rows - 1),
            dma(cols - 1),
            dma(cols - 1),
        ],
        compiler_params=pltpu.CompilerParams(
            collective_id=1, has_side_effects=True, vmem_limit_bytes=52 * 2**20
        ),
        cost_estimate=pl.CostEstimate(
            flops=20 * flops, bytes_accessed=200 * 2**20, transcendentals=0
        ),
    )(
        x, wide_x, wide_h, n_first, n_second, inv_first, inv_second, sym, hidden,
        taps(conv_first, True), taps(conv_second, True), w_head.T,
    )
    inverse_len = 1.0 / length
    flat = gathered.reshape(cols * depth, 256) * inverse_len

    def kernel_grad(base):
        part = flat[base : base + 3 * channels, : 3 * channels]
        part = part.reshape(3, channels, 3, channels).transpose(2, 0, 1, 3)
        return part.reshape(9, channels, channels)

    start = 6 * channels
    return (
        logits,
        grad_x.reshape(channels, height, lanes),
        kernel_grad(0),
        kernel_grad(3 * channels),
        flat[start : start + bins, :channels],
        flat[start : start + bins, 128],
    )


def solution(mesh):
    placed = (P(None, "col", "row"), P(), P(), P(), P(), P(None, "col", "row"))
    return jax.shard_map(
        on_device,
        mesh=mesh,
        in_specs=placed,
        out_specs=(P(None, "col", "row"), P(None, "col", "row"), P(), P(), P(), P()),
        check_vma=False,
    )
```

profile of v0, /device:TPU:0, one launch (start us, length us, event | category | flops | bytes accessed | tf_op | source)
XLA Modules:
  0.0 321.2 jit_solution(17823108550591654612)
XLA Ops:
  0.6 2.7 reshape.72
  3.3 4.7 %constant_dynamic-slice_fusion = (bf16[37,64,1,64]{3,2,1,0:T(2,128)(2,1)S(1)}, bf16[37,64,1,64]{3,2,1,0:T(2,128)(2,1)}) fusion(bf16[37,64,2,64]{3,2,1,0:T(2,128)(2,1)S(1)} %reshape.72, s32[]{:T(128)S(6)} %select_n.18, s32[]{:T(128)S(6)} %select_n.17), kind=kLoop, calls=%fused_computation.23 | loop fusion | bytes 1212424 | tf_op jit(solution)/shard_map/dynamic-slice.3
  8.0 3.5 %copy.57 = bf16[37,64,1,64]{1,3,0,2:T(8,128)(2,1)} copy(bf16[37,64,1,64]{3,2,1,0:T(2,128)(2,1)} %get-tuple-element.29) | data formatting | bytes 606208
  11.6 6.5 %collective-permute-start.2 = (bf16[37,64,64]{2,1,0:T(8,128)(2,1)}, bf16[37,64,64]{2,1,0:T(8,128)(2,1)}, u32[]{:S(2)}, u32[]{:S(2)}) collective-permute-start(bf16[37,64,64]{2,1,0:T(8,128)(2,1)} %bitcast.17), channel_id=1, source_target_pairs={{0,0},{1,1},{2,8},{3,9},{4,16},{5,17},{6,24},{7,25},{8,2},{9,3},{1... | collective-permute-start | bytes 909320 | tf_op jit(solution)/shard_map/ppermute | solution.py:82
  18.1 2.3 copy.58
  20.4 0.5 collective-permute-start.3
  20.8 0.0 copy-done.13
  20.8 0.1 copy.41
  20.9 0.1 copy.64
  21.0 0.0 copy-done.9
  21.0 0.2 copy.39
  21.2 0.1 copy.42.refs_1_
  21.3 0.0 copy-done.10
  21.3 0.1 copy.40
  21.5 0.0 copy-start.14
  21.5 0.1 copy.43.refs_2_
  21.6 0.0 copy-done.7
  21.6 0.7 copy.65
  22.3 0.0 copy-done.11
  22.4 0.0 copy-start
  22.4 0.1 broadcast_in_dim.2.refs_4_
  22.5 120.1 %shard_map.109 = (bf16[192,12288]{1,0:T(8,128)(2,1)S(1)}, bf16[192,12288]{1,0:T(8,128)(2,1)}, f32[64,8192]{1,0:T(8,128)S(1)}, f32[64,8192]{1,0:T(8,128)S(1)}, f3...) custom-call(bf16[64,8192]{1,0:T(8,128)(2,1)S(1)} %bitcast.59, ...), custom_call_target="tpu_custom_call" | custom-call | flops 12079595520 | bytes 209715200 | tf_op jit(solution)/shard_map/pallas_call | solution.py:532
  142.6 2.2 copy-done.1
  144.8 1.3 copy-done.2
  146.1 1.4 copy-done.3
  147.5 1.0 copy-done.4
  148.5 0.1 slice.42
  148.6 1.3 convert_element_type.29
  149.9 4.2 %constant_dynamic-slice_fusion.2 = (bf16[37,64,1,64]{3,2,1,0:T(2,128)(2,1)}, bf16[37,64,1,64]{3,2,1,0:T(2,128)(2,1)}) fusion(bf16[37,64,2,64]{3,2,1,0:T(2,128)(2,1)S(1)} %convert_element_type.29, s32[]{:T(128)S(6)} %select_n.18, s32[]{:T(128)S(6)} %select_n.17), kind=kLoop, calls=%fused_computation.25 | loop fusion | bytes 1212424 | tf_op jit(solution)/shard_map/dynamic-slice.1
  154.1 3.1 copy.55
  157.1 1.5 collective-permute-start
  158.7 0.0 copy-done.5
  158.7 2.3 copy.56
  161.0 0.1 collective-permute-start.1
  161.1 0.7 fusion.12
  164.4 1.6 copy.49
  166.0 1.6 copy.50
  167.6 0.1 slice.23
  167.7 0.9 rev.6
  168.6 0.1 copy.51.refs_9_
  168.7 0.9 rev.7
  169.7 0.1 copy.52.refs_10_
  169.8 0.0 copy-start.12
  169.8 0.2 copy.60
  171.4 0.0 collective-permute-done.2
  171.4 0.0 collective-permute-done.3
  171.4 0.0 collective-permute-done
  171.4 0.0 collective-permute-done.1
  171.5 0.0 copy-start.6
  171.5 2.9 fusion.5
  174.3 0.0 copy-done.6
  174.3 0.5 multiply_convert_fusion
  174.8 0.1 pad.23
  174.9 0.4 copy.61
  175.3 0.1 pad.14.refs_7_
  175.4 140.2 %shard_map.110 = (bf16[64,8192]{1,0:T(8,128)(2,1)}, f32[8,56,256]{2,1,0:T(8,128)S(1)}) custom-call(bf16[64,8192]{1,0:T(8,128)(2,1)} %bitcast.60, bf16[192,12288]{1,0:T(8,128)(2,1)} %copy-done.1, bf16[192,12288]{1,0:T(8,128)(2,1)} %get-tuple-element.18.refs_2_, f32[64,8192]{1,0:T(8,128)} %copy-done.2, f32[64,8192]{1,0:T(8,128)} %copy-done.3, ...), custom_call_target="tpu_custom_call" | custom-call | flops 12079595520 | bytes 209715200 | tf_op jit(solution)/shard_map/pallas_call | solution.py:565
  315.6 0.6 slice_reduce_fusion
  316.2 0.6 slice.32
  316.9 1.3 copy.62
  318.1 0.2 reshape.79
  318.3 0.7 copy.54
  319.1 0.2 reshape.77
  319.2 0.7 copy.53
  320.0 1.2 fusion.1
  (21 shorter events, 0.1 us)
Async XLA Ops:
  11.6 9.3 %copy-start.13 = (bf16[37,64]{1,0:T(8,128)(2,1)S(1)}, bf16[37,64]{1,0:T(8,128)(2,1)}, u32[]{:S(2)}) copy-start(bf16[37,64]{1,0:T(8,128)(2,1)} %param.9) | copy-start | bytes 14212
  11.6 9.5 %copy-start.9 = (bf16[9,64,64]{2,1,0:T(8,128)(2,1)S(1)}, bf16[9,64,64]{2,1,0:T(8,128)(2,1)}, u32[]{:S(2)}) copy-start(bf16[9,64,64]{2,1,0:T(8,128)(2,1)} %param.7) | copy-start | bytes 221188
  11.6 9.8 %copy-start.10 = (bf16[9,64,64]{2,1,0:T(8,128)(2,1)S(1)}, bf16[9,64,64]{2,1,0:T(8,128)(2,1)}, u32[]{:S(2)}) copy-start(bf16[9,64,64]{2,1,0:T(8,128)(2,1)} %param.8) | copy-start | bytes 221188
  11.6 159.8 %collective-permute-start.2 = (bf16[37,64,64]{2,1,0:T(8,128)(2,1)}, bf16[37,64,64]{2,1,0:T(8,128)(2,1)}, u32[]{:S(2)}, u32[]{:S(2)}) collective-permute-start(bf16[37,64,64]{2,1,0:T(8,128)(2,1)} %bitcast.17), channel_id=1, source_target_pairs={{0,0},{1,1},{2,8},{3,9},{4,16},{5,17},{6,24},{7,25},{8,2},{9,3},{1... | collective-permute-start | bytes 909320 | tf_op jit(solution)/shard_map/ppermute | solution.py:82
  18.1 3.6 %copy-start.7 = (bf16[64,64,128]{2,1,0:T(8,128)(2,1)S(1)}, bf16[64,64,128]{2,1,0:T(8,128)(2,1)}, u32[]{:S(2)}) copy-start(bf16[64,64,128]{2,1,0:T(8,128)(2,1)} %param.6) | copy-start | bytes 3145732
  20.4 151.0 %collective-permute-start.3 = (bf16[37,64,64]{2,1,0:T(8,128)(2,1)}, bf16[37,64,64]{2,1,0:T(8,128)(2,1)}, u32[]{:S(2)}, u32[]{:S(2)}) collective-permute-start(bf16[37,64,64]{2,1,0:T(8,128)(2,1)} %bitcast.20), channel_id=1, source_target_pairs={{0,1},{1,0},{2,9},{3,8},{4,17},{5,16},{6,25},{7,24},{8,3},{9,2},{1... | collective-permute-start | bytes 909320 | tf_op jit(solution)/shard_map/ppermute | solution.py:82
  20.9 1.4 copy-start.11
  21.5 0.9 copy-start.14
  22.4 120.2 %copy-start = (bf16[8,8,64,128]{3,1,2,0:T(8,128)(2,1)}, bf16[8,8,64,128]{3,1,2,0:T(8,128)(2,1)S(1)}, u32[]{:S(2)}) copy-start(bf16[8,8,64,128]{3,1,2,0:T(8,128)(2,1)S(1)} %copy.65) | copy-start | bytes 3145732
  142.6 2.2 copy-start.1
  144.8 1.3 copy-start.2
  146.1 1.4 copy-start.3
  147.5 1.0 copy-start.4
  154.1 4.6 %copy-start.5 = (bf16[37,64,1,64]{3,2,1,0:T(2,128)(2,1)S(1)}, bf16[37,64,1,64]{3,2,1,0:T(2,128)(2,1)}, u32[]{:S(2)}) copy-start(bf16[37,64,1,64]{3,2,1,0:T(2,128)(2,1)} %get-tuple-element.32) | copy-start | bytes 909316
  157.1 14.3 %collective-permute-start = (bf16[37,64,64]{2,1,0:T(8,128)(2,1)S(1)}, bf16[37,64,64]{2,1,0:T(8,128)(2,1)}, u32[]{:S(2)}, u32[]{:S(2)}) collective-permute-start(bf16[37,64,64]{2,1,0:T(8,128)(2,1)S(1)} %bitcast.73), channel_id=1, source_target_pairs={{0,0},{1,1},{2,8},{3,9},{4,16},{5,17},{6,24},{7,25},{8,2},{9,3},{1... | collective-permute-start | bytes 909320 | tf_op jit(solution)/shard_map/ppermute | solution.py:82
  161.0 10.5 %collective-permute-start.1 = (bf16[37,64,64]{2,1,0:T(8,128)(2,1)}, bf16[37,64,64]{2,1,0:T(8,128)(2,1)}, u32[]{:S(2)}, u32[]{:S(2)}) collective-permute-start(bf16[37,64,64]{2,1,0:T(8,128)(2,1)} %bitcast.74), channel_id=1, source_target_pairs={{0,1},{1,0},{2,9},{3,8},{4,17},{5,16},{6,25},{7,24},{8,3},{9,2},{1... | collective-permute-start | bytes 909320 | tf_op jit(solution)/shard_map/ppermute | solution.py:82
  169.8 1.6 copy-start.12
  171.5 2.9 copy-start.6
  315.6 1.3 copy-start.8
where the time goes:
time: 324 us; the launch traced here: 321 us
  Pallas kernels  260 us (80%)
  local copies, waits for them, and re-layouts  42.7 us (13%)
  starting transfers between devices  8.57 us (3%)
  between operations  5.02 us (2%)
  other arithmetic  4.6 us (1%)
    pallas_call x1, Pallas kernels, on_device(): pl.pallas_call(functools.partial(backward_kernel, plan, cell_count, depth...  140 us
    pallas_call x1, Pallas kernels, on_device(): pl.pallas_call(functools.partial(forward_kernel, plan, cell_count), out_s...  120 us
    unnamed x41, local copies, waits for them, and re-layouts  20 us
    another operation x2, local copies, waits for them, and re-layouts  8.89 us
    ppermute x4, starting transfers between devices, mirror(): arrived.append(lax.ppermute(mine, ('row', 'col'), pairs))  8.57 us
  transfers between devices with their start and end apart: 4, of which 0 were waited for; matrix products, arithmetic and copies ran while one was open for 7% of the time, Pallas kernels for 37%

commit v1 on v0

--- a/solution.py
+++ b/solution.py
@@ -65,27 +65,98 @@
     return total
 
 
-def mirror(tensor):
-    rows, cols = lax.axis_size("row"), lax.axis_size("col")
-    ratio = cols // rows
-    edge = tensor.shape[1]
-    col = lax.axis_index("col")
-    halves = tensor.reshape(tensor.shape[0], edge, ratio, edge).transpose(2, 0, 3, 1)
-    arrived = []
-    for step in range(ratio):
-        pairs = [
-            (r * cols + c, (c // ratio) * cols + ratio * r + (c + step) % ratio)
-            for r in range(rows)
-            for c in range(cols)
-        ]
-        mine = lax.dynamic_index_in_dim(halves, lax.rem(col + step, ratio), 0, False)
-        arrived.append(lax.ppermute(mine, ("row", "col"), pairs))
-    stacked = jnp.stack(arrived)
-    places = lax.rem(col - jnp.arange(ratio) + ratio * cols, ratio)
-    ordered = [
-        lax.dynamic_index_in_dim(stacked, places[index], 0, False) for index in range(ratio)
-    ]
-    return jnp.concatenate(ordered, axis=2)
+def mirror_pack(tensor, rows):
+    planes, edge, lanes = tensor.shape
+    each = -(-planes // rows)
+    halves = lanes // edge
+    padded = jnp.pad(tensor, ((0, each * rows - planes), (0, 0), (0, 0)))
+    turned = padded.reshape(rows, each, edge, halves, edge).transpose(0, 3, 1, 4, 2)
+    return turned.reshape(rows, halves, each, edge * edge // 128, 128)
+
+
+def mirror_unpack(arrived, planes, edge):
+    rows, halves, each = arrived.shape[:3]
+    turned = arrived.reshape(rows, halves, each, edge, edge).transpose(0, 2, 3, 1, 4)
+    return turned.reshape(rows * each, edge, halves * edge)[:planes]
+
+
+class Mirror:
+    def __init__(self, rows, cols, source, landing, refs):
+        self.rows, self.cols = rows, cols
+        self.source, self.landing = source, landing
+        self.first, self.second = refs[:2]
+        self.sems = refs[2:]
+        self.ratio = cols // rows
+        self.copies = None
+
+    def hop_one(self):
+        row = lax.axis_index("row")
+        self.first[row] = self.source[row]
+        self.copies = share(
+            "row", self.rows, lambda t: self.source.at[t], self.first, *self.sems[0:2]
+        )
+
+    def hop_two(self):
+        finish(self.copies)
+        col, ratio = lax.axis_index("col"), self.ratio
+        self.second[col] = self.first[lax.div(col, ratio), lax.rem(col, ratio)]
+        self.copies = share(
+            "col",
+            self.cols,
+            lambda t: self.first.at[lax.div(t, ratio), lax.rem(t, ratio)],
+            self.second,
+            *self.sems[2:4],
+        )
+
+    def hop_three(self):
+        finish(self.copies)
+        row, ratio = lax.axis_index("row"), self.ratio
+        self.landing[row] = self.second[pl.ds(row * ratio, ratio)]
+        self.copies = share(
+            "row",
+            self.rows,
+            lambda t: self.second.at[pl.ds(t * ratio, ratio)],
+            self.landing,
+            *self.sems[4:6],
+        )
+
+    def end(self):
+        finish(self.copies)
+
+
+class WeightSum:
+    def __init__(self, rows, cols, depth, refs):
+        self.rows, self.cols, self.depth = rows, cols, depth
+        self.mine, self.parts, self.over_row, self.whole = refs[:4]
+        self.sems = refs[4:]
+        self.copies = None
+
+    def piece(self, t):
+        return self.mine.at[pl.ds(pl.multiple_of(t * self.depth, 8), self.depth)]
+
+    def scatter(self):
+        col = lax.axis_index("col")
+        self.parts[col] = self.piece(col)[...]
+        self.copies = share("col", self.cols, self.piece, self.parts, *self.sems[0:2])
+
+    def across(self):
+        finish(self.copies)
+        row = lax.axis_index("row")
+        self.over_row[row] = in_order(self.parts, self.cols)
+        self.copies = share(
+            "row", self.rows, lambda t: self.over_row.at[row], self.over_row, *self.sems[2:4]
+        )
+
+    def gather(self):
+        finish(self.copies)
+        col = lax.axis_index("col")
+        self.whole[col] = in_order(self.over_row, self.rows)
+        self.copies = share(
+            "col", self.cols, lambda t: self.whole.at[col], self.whole, *self.sems[4:6]
+        )
+
+    def end(self):
+        finish(self.copies)
 
 
 def dma(count):
@@ -142,6 +213,35 @@
         return [
             pltpu.VMEM((self.rows, 8, 128), jnp.float32),
             pltpu.VMEM((self.cols, 8, 128), jnp.float32),
+            dma(self.rows - 1),
+            dma(self.rows - 1),
+            dma(self.cols - 1),
+            dma(self.cols - 1),
+        ]
+
+    def mirror_scratch(self, packed):
+        return [
+            pltpu.VMEM(packed.shape, jnp.bfloat16),
+            pltpu.VMEM((self.cols, *packed.shape[2:]), jnp.bfloat16),
+            dma(self.rows - 1),
+            dma(self.rows - 1),
+            dma(self.cols - 1),
+            dma(self.cols - 1),
+            dma(self.rows - 1),
+            dma(self.rows - 1),
+        ]
+
+    def depth(self, count):
+        return -(-count // (self.cols * 8)) * 8
+
+    def weight_scratch(self, depth):
+        return [
+            pltpu.VMEM((self.cols * depth, 256), jnp.float32),
+            pltpu.VMEM((self.cols, depth, 256), jnp.float32),
+            pltpu.VMEM((self.rows, depth, 256), jnp.float32),
+            pltpu.VMEM((self.cols, depth, 256), jnp.float32),
+            dma(self.cols - 1),
+            dma(self.cols - 1),
             dma(self.rows - 1),
             dma(self.rows - 1),
             dma(self.cols - 1),
@@ -326,16 +426,20 @@
 
 
 def forward_kernel(plan, cell_count, *refs):
-    x, w_first, w_second, w_head, bias = refs[:5]
-    wide_x, wide_h, n_first, n_second, raw, hidden, inv_first, inv_second = refs[5:13]
-    act = refs[13]
-    ends_x, ends_h = refs[14:20], refs[20:26]
-    sums_first, sums_second = refs[26:32], refs[32:38]
+    x, k_first, k_second, w_head, bias, turned = refs[:6]
+    wide_x, wide_h, n_first, n_second, raw, hidden, inv_first, inv_second, landing = refs[6:15]
+    act, w_first, w_second = refs[15:18]
+    ends_x, ends_h = refs[18:24], refs[24:30]
+    sums_first, sums_second = refs[30:36], refs[36:42]
+    mirror = Mirror(plan.rows, plan.cols, turned, landing, refs[42:50])
     n = plan.channels
     zero = jnp.zeros((n, 1), jnp.float32)
     clear(plan, wide_x, ends_x[2], ends_x[3])
     clear(plan, wide_h, ends_h[2], ends_h[3])
     meet(plan.rows, plan.cols)
+    mirror.hop_one()
+    build_taps(k_first, w_first, False)
+    build_taps(k_second, w_second, False)
 
     def load(index, carry):
         emit(plan, wide_x, ends_x[0], ends_x[1], index, x[:, plan.at(index)].astype(jnp.float32))
@@ -364,6 +468,7 @@
         return average, inverse
 
     average, inverse = moments(convolve(wide_x, w_first), sums_first, inv_first)
+    mirror.hop_two()
 
     def middle(index, carry):
         normed = (act[:, plan.at(index)] - average) * inverse
@@ -375,6 +480,7 @@
     copies = halo_copies(plan, wide_h, *ends_h)
     halo_start(copies)
     halo_wait(copies)
+    mirror.hop_three()
     mend(plan, wide_h, ends_h[2], ends_h[3])
     average_2, inverse_2 = moments(convolve(wide_h, w_second), sums_second, inv_second)
 
@@ -390,25 +496,30 @@
         return carry
 
     lax.fori_loop(0, plan.chunks, tail, 0)
-
-
-def backward_kernel(plan, cell_count, depth, *refs):
+    mirror.end()
+
+
+def backward_kernel(plan, cell_count, depths, *refs):
     (x, wide_x, wide_h, n_first, n_second, inv_first, inv_second) = refs[:7]
-    sym, hidden, w_first, w_second, w_head = refs[7:12]
-    grad_x, gathered = refs[12:14]
-    wide_2, wide_1, slope_grad, inner_grad = refs[14:18]
-    ends_2, ends_1 = refs[18:24], refs[24:30]
-    sums_2, sums_1 = refs[30:36], refs[36:42]
-    (mine, parts, over_row, whole, part_out, part_in) = refs[42:48]
-    row_out, row_in, col_out, col_in = refs[48:52]
-    row, col = lax.axis_index("row"), lax.axis_index("col")
+    sym, hidden, k_first, k_second, w_head, turned = refs[7:13]
+    grad_x, sum_first, sum_second, landing = refs[13:17]
+    wide_2, wide_1, slope_grad, inner_grad, w_first, w_second = refs[17:23]
+    ends_2, ends_1 = refs[23:29], refs[29:35]
+    sums_2, sums_1 = refs[35:41], refs[41:47]
+    late = WeightSum(plan.rows, plan.cols, depths[0], refs[47:57])
+    early = WeightSum(plan.rows, plan.cols, depths[1], refs[57:67])
+    mirror = Mirror(plan.rows, plan.cols, turned, landing, refs[67:75])
     n, bins = plan.channels, sym.shape[0]
     zero = jnp.zeros((n, 1), jnp.float32)
     clear(plan, wide_2, ends_2[2], ends_2[3])
     clear(plan, wide_1, ends_1[2], ends_1[3])
-    mine[...] = jnp.zeros_like(mine)
+    late.mine[...] = jnp.zeros_like(late.mine)
+    early.mine[...] = jnp.zeros_like(early.mine)
     meet(plan.rows, plan.cols)
-    head_at = 6 * n
+    mirror.hop_one()
+    build_taps(k_first, w_first, True)
+    build_taps(k_second, w_second, True)
+    head_at = 3 * n
 
     def start(index, carry):
         place = plan.at(index)
@@ -417,11 +528,11 @@
         part = jnp.dot(w_head[...], sym_part, preferred_element_type=jnp.float32)
         part = part * elu_slope(summed)
         slope_grad[:, place] = part
-        mine[head_at : head_at + bins, 0:n] += lax.dot_general(
+        early.mine[head_at : head_at + bins, 0:n] += lax.dot_general(
             sym_part, hidden[:, place], (((1,), (1,)), ((), ())),
             preferred_element_type=jnp.float32,
         )
-        mine[head_at : head_at + bins, 128:256] += jnp.broadcast_to(
+        early.mine[head_at : head_at + bins, 128:256] += jnp.broadcast_to(
             jnp.sum(sym_part.astype(jnp.float32), axis=1, keepdims=True), (bins, 128)
         )
         found = pair_of(part, part * n_second[:, place])
@@ -429,8 +540,9 @@
 
     pair = lax.fori_loop(0, plan.chunks, start, (zero, zero))
 
-    def step_back(pair, scratch, source, normed, inverse_ref, wide, ends):
+    def step_back(pair, scratch, source, normed, inverse_ref, wide, ends, beside):
         first_sum, second_sum = total_sums(plan, pair, *scratch)
+        beside()
         first_mean, second_mean = first_sum / cell_count, second_sum / cell_count
         inverse = inverse_ref[:, 0:1]
 
@@ -445,18 +557,22 @@
         halo_start(copies)
         return copies
 
-    def weigh(wide, against, base):
+    def weigh(wide, against, table):
         def body(index, carry):
             gradient = wide[n : 2 * n, plan.at(index, plan.margin)]
             for b, part in enumerate(weight_chunk(plan, against, gradient, index)):
-                mine[base + b * n : base + (b + 1) * n, 0 : 3 * n] += part
+                table.mine[b * n : (b + 1) * n, 0 : 3 * n] += part
             return carry
 
         lax.fori_loop(0, plan.chunks, body, 0)
 
-    copies = step_back(pair, sums_2, slope_grad, n_second, inv_second, wide_2, ends_2)
-    weigh(wide_2, wide_h, 3 * n)
+    copies = step_back(
+        pair, sums_2, slope_grad, n_second, inv_second, wide_2, ends_2, mirror.hop_two
+    )
+    weigh(wide_2, wide_h, early)
     halo_wait(copies)
+    mirror.hop_three()
+    early.scatter()
     mend(plan, wide_2, ends_2[2], ends_2[3])
 
     def through(index, carry):
@@ -468,19 +584,14 @@
         return carry[0] + found[0], carry[1] + found[1]
 
     pair = lax.fori_loop(0, plan.chunks, through, (zero, zero))
-    copies = step_back(pair, sums_1, inner_grad, n_first, inv_first, wide_1, ends_1)
-    weigh(wide_1, wide_x, 0)
-
-    def piece(ref, t):
-        return ref.at[pl.ds(pl.multiple_of(t * depth, 8), depth)]
-
-    parts[col] = piece(mine, col)[...]
-    sums = share("col", plan.cols, lambda t: piece(mine, t), parts, part_out, part_in)
+    early.across()
+    copies = step_back(
+        pair, sums_1, inner_grad, n_first, inv_first, wide_1, ends_1, early.gather
+    )
+    weigh(wide_1, wide_x, late)
     halo_wait(copies)
+    late.scatter()
     mend(plan, wide_1, ends_1[2], ends_1[3])
-    finish(sums)
-    over_row[row] = in_order(parts, plan.cols)
-    sums = share("row", plan.rows, lambda t: over_row.at[row], over_row, row_out, row_in)
 
     def last(index, carry):
         place = plan.at(index)
@@ -488,23 +599,32 @@
         grad_x[:, place] = part.astype(jnp.bfloat16)
         return carry
 
-    lax.fori_loop(0, plan.chunks, last, 0)
-    finish(sums)
-    whole[col] = in_order(over_row, plan.rows)
-    finish(share("col", plan.cols, lambda t: whole.at[col], whole, col_out, col_in))
-    gathered[...] = whole[...]
+    half = plan.chunks // 2
+    lax.fori_loop(0, half, last, 0)
+    late.across()
+    lax.fori_loop(half, plan.chunks, last, 0)
+    late.gather()
+    early.end()
+    mirror.end()
+    sum_second[...] = early.whole[...]
+    late.end()
+    sum_first[...] = late.whole[...]
 
 
 def vmem(count):
     return [pl.BlockSpec(memory_space=pltpu.VMEM)] * count
 
 
-def taps(weights, adjoint):
-    count, outs, ins = weights.shape
-    grid = weights.reshape(3, 3, outs, ins)
-    if adjoint:
-        return grid[::-1, ::-1].transpose(1, 3, 0, 2).reshape(3, ins, 3 * outs)
-    return grid.transpose(1, 2, 0, 3).reshape(3, outs, 3 * ins)
+def build_taps(kernel, table, adjoint):
+    for b in range(3):
+        parts = []
+        for a in range(3):
+            if adjoint:
+                part = kernel[3 * (2 - a) + 2 - b].astype(jnp.float32).T
+            else:
+                part = kernel[3 * a + b].astype(jnp.float32)
+            parts.append(part)
+        table[b] = jnp.concatenate(parts, axis=1).astype(jnp.bfloat16)
 
 
 def on_device(features, conv_first, conv_second, head_weight, head_bias, cotangent):
@@ -516,11 +636,6 @@
     padded = -(-bins // 16) * 16
     plan = Plan(channels, height, lanes, rows, cols)
     cells, width = plan.cells, plan.width
-    cot_mirror = mirror(cotangent)
-    grad_sym = (0.5 * (cotangent.astype(jnp.float32) + cot_mirror.astype(jnp.float32))).astype(
-        jnp.bfloat16
-    )
-    sym = jnp.pad(grad_sym.reshape(bins, cells), ((0, padded - bins), (0, 0)))
     x = features.reshape(channels, cells)
     w_head = jnp.pad(head_weight, ((0, padded - bins), (0, 0)))
     bias = jnp.broadcast_to(jnp.pad(head_bias, (0, padded - bins))[:, None], (padded, 128))
@@ -529,7 +644,10 @@
     short_shape = jax.ShapeDtypeStruct((channels, cells), jnp.bfloat16)
     inverse_shape = jax.ShapeDtypeStruct((channels, 128), jnp.float32)
     flops = 2 * 9 * channels * channels * cells
-    wide_x, wide_h, n_first, n_second, raw, hidden, inv_first, inv_second = pl.pallas_call(
+    turned = mirror_pack(cotangent, rows)
+    landing_shape = jax.ShapeDtypeStruct(turned.shape, jnp.bfloat16)
+    taps_scratch = pltpu.VMEM((3, channels, 3 * channels), jnp.bfloat16)
+    wide_x, wide_h, n_first, n_second, raw, hidden, inv_first, inv_second, arrived = pl.pallas_call(
         functools.partial(forward_kernel, plan, cell_count),
         out_shape=(
             wide_shape,
@@ -540,15 +658,19 @@
             short_shape,
             inverse_shape,
             inverse_shape,
+            landing_shape,
         ),
-        in_specs=vmem(5),
-        out_specs=tuple(vmem(8)),
+        in_specs=vmem(6),
+        out_specs=tuple(vmem(9)),
         scratch_shapes=[
             pltpu.VMEM((channels, cells), jnp.float32),
+            taps_scratch,
+            taps_scratch,
             *plan.wide_scratch(),
             *plan.wide_scratch(),
             *plan.sum_scratch(),
             *plan.sum_scratch(),
+            *plan.mirror_scratch(turned),
         ],
         compiler_params=pltpu.CompilerParams(
             collective_id=0, has_side_effects=True, vmem_limit_bytes=40 * 2**20
@@ -556,36 +678,35 @@
         cost_estimate=pl.CostEstimate(
             flops=20 * flops, bytes_accessed=200 * 2**20, transcendentals=0
         ),
-    )(x, taps(conv_first, False), taps(conv_second, False), w_head, bias)
+    )(x, conv_first, conv_second, w_head, bias, turned)
+    cot_mirror = mirror_unpack(arrived, bins, height)
+    grad_sym = (0.5 * (cotangent.astype(jnp.float32) + cot_mirror.astype(jnp.float32))).astype(
+        jnp.bfloat16
+    )
+    sym = jnp.pad(grad_sym.reshape(bins, cells), ((0, padded - bins), (0, 0)))
     raw_logits = raw[:bins].reshape(bins, height, lanes)
-    logit_mirror = mirror(raw_logits.astype(jnp.bfloat16)).astype(jnp.float32)
-    logits = (0.5 * (raw_logits + logit_mirror)).astype(jnp.bfloat16)
-    total_rows = 6 * channels + padded
-    depth = -(-total_rows // (cols * 8)) * 8
-    grad_x, gathered = pl.pallas_call(
-        functools.partial(backward_kernel, plan, cell_count, depth),
-        out_shape=(short_shape, jax.ShapeDtypeStruct((cols, depth, 256), jnp.float32)),
-        in_specs=vmem(12),
-        out_specs=tuple(vmem(2)),
+    turned = mirror_pack(raw_logits.astype(jnp.bfloat16), rows)
+    depths = (plan.depth(3 * channels), plan.depth(3 * channels + padded))
+    sum_shapes = [jax.ShapeDtypeStruct((cols, depth, 256), jnp.float32) for depth in depths]
+    grad_x, sum_first, sum_second, arrived = pl.pallas_call(
+        functools.partial(backward_kernel, plan, cell_count, depths),
+        out_shape=(short_shape, *sum_shapes, landing_shape),
+        in_specs=vmem(13),
+        out_specs=tuple(vmem(4)),
         scratch_shapes=[
             pltpu.VMEM(wide_shape.shape, jnp.bfloat16),
             pltpu.VMEM(wide_shape.shape, jnp.bfloat16),
             pltpu.VMEM((channels, cells), jnp.float32),
             pltpu.VMEM((channels, cells), jnp.float32),
+            taps_scratch,
+            taps_scratch,
             *plan.wide_scratch(),
             *plan.wide_scratch(),
             *plan.sum_scratch(),
             *plan.sum_scratch(),
-            pltpu.VMEM((cols * depth, 256), jnp.float32),
-            pltpu.VMEM((cols, depth, 256), jnp.float32),
-            pltpu.VMEM((rows, depth, 256), jnp.float32),
-            pltpu.VMEM((cols, depth, 256), jnp.float32),
-            dma(cols - 1),
-            dma(cols - 1),
-            dma(rows - 1),
-            dma(rows - 1),
-            dma(cols - 1),
-            dma(cols - 1),
+            *plan.weight_scratch(depths[0]),
+            *plan.weight_scratch(depths[1]),
+            *plan.mirror_scratch(turned),
         ],
         compiler_params=pltpu.CompilerParams(
             collective_id=1, has_side_effects=True, vmem_limit_bytes=52 * 2**20
@@ -595,24 +716,26 @@
         ),
     )(
         x, wide_x, wide_h, n_first, n_second, inv_first, inv_second, sym, hidden,
-        taps(conv_first, True), taps(conv_second, True), w_head.T,
+        conv_first, conv_second, w_head.T, turned,
     )
+    logit_mirror = mirror_unpack(arrived, bins, height).astype(jnp.float32)
+    logits = (0.5 * (raw_logits + logit_mirror)).astype(jnp.bfloat16)
     inverse_len = 1.0 / length
-    flat = gathered.reshape(cols * depth, 256) * inverse_len
-
-    def kernel_grad(base):
-        part = flat[base : base + 3 * channels, : 3 * channels]
+
+    def kernel_grad(table):
+        part = table[: 3 * channels, : 3 * channels] * inverse_len
         part = part.reshape(3, channels, 3, channels).transpose(2, 0, 1, 3)
         return part.reshape(9, channels, channels)
 
-    start = 6 * channels
+    sum_first, sum_second = sum_first.reshape(-1, 256), sum_second.reshape(-1, 256)
+    head = sum_second[3 * channels : 3 * channels + bins] * inverse_len
     return (
         logits,
         grad_x.reshape(channels, height, lanes),
-        kernel_grad(0),
-        kernel_grad(3 * channels),
-        flat[start : start + bins, :channels],
-        flat[start : start + bins, 128],
+        kernel_grad(sum_first),
+        kernel_grad(sum_second),
+        head[:, :channels],
+        head[:, 128],
     )
 
 

time: 324 us -> 201 us (0.62)
  Pallas kernels: 260 us -> 158 us
  starting transfers between devices: 8.57 us -> 0 us
  between operations: 5.02 us -> 0.89 us
  other arithmetic: 4.6 us -> 1.29 us
    pallas_call x1, Pallas kernels: 140 us -> 85.7 us  [on_device(): pl.pallas_call(functools.partial(backward_kernel, plan, cell_count, depth...]
    pallas_call x1, Pallas kernels: 120 us -> 72.1 us  [on_device(): pl.pallas_call(functools.partial(forward_kernel, plan, cell_count), out_s...]
    reshape x9 -> x11, local copies, waits for them, and re-layouts: 6.65 us -> 17.6 us  [the longest x4 6.34 us: mirror_pack(): padded.reshape(rows, each, edge, halves, edge).transpose(0, 3, 1, 4, 2)]
    another operation x2 -> x0, local copies, waits for them, and re-layouts: 8.89 us -> none
    ppermute x4 -> x0, starting transfers between devices: 8.57 us -> none  [mirror(): arrived.append(lax.ppermute(mine, ('row', 'col'), pairs))]
    unnamed x41 -> x29, local copies, waits for them, and re-layouts: 20 us -> 12 us
    transpose x1 -> x3, local copies, waits for them, and re-layouts: 0.01 us -> 4.86 us  [the longest x2 4.85 us: mirror_unpack(): arrived.reshape(rows, halves, each, edge, edge).transpose(0, 2, 3, 1, 4)]
  transfers between devices with their start and end apart: 4 -> 0, of which waited for: 0 -> 0; matrix products, arithmetic and copies ran while one was open for 7% -> 0% of each run, Pallas kernels for 37% -> 0%
where the time goes in v1:
time: 201 us; the launch traced here: 200 us
  Pallas kernels  158 us (79%)
  local copies, waits for them, and re-layouts  40.4 us (20%)
    pallas_call x1, Pallas kernels, on_device(): pl.pallas_call(functools.partial(backward_kernel, plan, cell_count, depth...  85.7 us
    pallas_call x1, Pallas kernels, on_device(): pl.pallas_call(functools.partial(forward_kernel, plan, cell_count), out_s...  72.1 us
    unnamed x29, local copies, waits for them, and re-layouts  12 us
    reshape x4, local copies, waits for them, and re-layouts, mirror_pack(): padded.reshape(rows, each, edge, halves, edge).transpose(0, 3, 1, 4, 2)  6.34 us
    reshape x2, local copies, waits for them, and re-layouts, mirror_unpack(): return turned.reshape(rows * each, edge, halves * edge)[:planes]  5.57 us
    transpose x2, local copies, waits for them, and re-layouts, mirror_unpack(): arrived.reshape(rows, halves, each, edge, edge).transpose(0, 2, 3, 1, 4)  4.85 us
    reshape x2, local copies, waits for them, and re-layouts, mirror_pack(): return turned.reshape(rows, halves, each, edge * edge // 128, 128)  4.61 us

profile of v1, /device:TPU:0, one launch (start us, length us, event | category | flops | bytes accessed | tf_op | source)
XLA Modules:
  0.0 200.4 jit_solution(16787661425944675252)
XLA Ops:
  0.6 0.7 pad.20
  1.3 0.8 copy.26
  2.1 0.1 copy.39
  2.2 0.1 broadcast_in_dim.2.refs_4_
  2.3 1.1 pad.21
  3.4 0.5 reshape.68
  3.9 2.7 %copy.27 = bf16[4,10,64,2,64]{2,4,1,3,0:T(8,128)(2,1)} copy(bf16[4,10,64,2,64]{4,3,2,1,0:T(2,128)(2,1)S(1)} %reshape.68) | data formatting | bytes 1310720 | tf_op jit(solution)/shard_map/reshape | solution.py:73
  6.6 0.0 copy-start.10
  6.6 2.0 reshape.69.refs_5_
  8.6 0.0 copy-done.10
  8.6 0.0 copy-start.1
  8.6 0.0 copy-start.2
  8.6 0.7 copy.40
  9.3 0.0 copy-start
  9.4 0.2 copy-done.1
  9.5 0.1 copy-done.2
  9.6 72.1 %shard_map.109 = (bf16[192,12288]{1,0:T(8,128)(2,1)S(1)}, bf16[192,12288]{1,0:T(8,128)(2,1)}, f32[64,8192]{1,0:T(8,128)S(1)}, f32[64,8192]{1,0:T(8,128)S(1)}, f3...) custom-call(bf16[64,8192]{1,0:T(8,128)(2,1)S(1)} %bitcast.32, ...), custom_call_target="tpu_custom_call" | custom-call | flops 12079595520 | bytes 209715200 | tf_op jit(solution)/shard_map/pallas_call | solution.py:650
  81.7 0.0 copy-done
  81.7 0.0 copy-start.3
  81.8 2.2 %copy-done.3 = bf16[192,12288]{1,0:T(8,128)(2,1)} copy-done((bf16[192,12288]{1,0:T(8,128)(2,1)}, bf16[192,12288]{1,0:T(8,128)(2,1)S(1)}, u32[]{:S(2)}) %copy-start.3) | copy-done | bytes 4718616
  84.0 0.0 copy-start.5
  84.0 1.3 copy-done.5
  85.3 0.0 copy-start.6
  85.3 1.0 copy-done.6
  86.3 0.0 copy-start.4
  86.3 0.1 slice.24
  86.4 1.2 copy-done.4
  87.6 0.2 copy.35
  87.9 0.0 copy-start.7
  87.9 1.1 copy-done.7
  89.0 0.1 slice.48
  89.1 0.1 pad.23
  89.1 0.5 reshape.74
  89.6 2.7 %copy.30 = bf16[4,10,64,2,64]{2,4,1,3,0:T(8,128)(2,1)} copy(bf16[4,10,64,2,64]{4,3,2,1,0:T(2,128)(2,1)S(1)} %reshape.74) | data formatting | bytes 1310720 | tf_op jit(solution)/shard_map/reshape | solution.py:73
  92.3 2.6 %reshape.75.refs_12_ = bf16[4,2,10,32,128]{4,3,2,1,0:T(8,128)(2,1)} reshape(bf16[4,2,10,64,64]{4,3,2,1,0:T(8,128)(2,1)} %bitcast.41) | data formatting | bytes 1310720 | tf_op jit(solution)/shard_map/reshape | solution.py:74
  94.9 0.5 reshape.71
  95.4 2.4 %copy.29 = bf16[4,10,64,2,64]{4,3,2,1,0:T(2,128)(2,1)} copy(bf16[4,10,64,2,64]{4,2,1,3,0:T(8,128)(2,1)S(1)} %bitcast.42) | data formatting | bytes 1310720 | tf_op jit(solution)/shard_map/transpose | solution.py:79
  97.9 0.0 copy-start.9
  97.9 2.8 %reshape.72 = bf16[40,64,128]{2,1,0:T(8,128)(2,1)S(1)} reshape(bf16[4,10,64,2,64]{4,3,2,1,0:T(2,128)(2,1)} %copy.29) | data formatting | bytes 1310720 | tf_op jit(solution)/shard_map/reshape | solution.py:80
  100.6 0.0 copy-done.9
  100.7 0.2 multiply_convert_fusion.1
  100.9 0.1 pad.24
  101.0 0.4 copy.36
  101.4 1.0 pad.22.refs_7_
  102.4 85.7 %shard_map.110 = (bf16[64,8192]{1,0:T(8,128)(2,1)}, f32[8,24,256]{2,1,0:T(8,128)S(1)}, f32[8,32,256]{2,1,0:T(8,128)S(1)}, bf16[4,2,10,32,128]{4,3,2,1,0:T(8,128)(2,1)S(1)}) custom-call(bf16[64,8192]{1,0:T(8,128)(2,1)} %bitcast.33, bf16[192,12288]{1,0:T(8,128)(2,1)} %copy-done.3, bf16[192,12288]{1,0:T(8,128)(2,1)} %get-tuple-element.21.refs_2_, ...), custom_call_target="tpu_custom_call" | custom-call | flops 12079595520 | bytes 209715200 | tf_op jit(solution)/shard_map/pallas_call | solution.py:691
  188.1 2.5 %copy.37 = bf16[8,8,64,128]{3,2,1,0:T(8,128)(2,1)} copy(bf16[8,8,64,128]{3,1,2,0:T(8,128)(2,1)} %bitcast.50) | data formatting | bytes 2097152
  190.6 0.6 slice_reduce_fusion
  191.2 0.6 slice.37
  191.8 0.2 reshape.83
  192.0 0.7 copy.33
  192.7 0.2 reshape.80
  192.9 0.7 copy.32
  193.7 0.5 reshape.76
  194.2 2.4 %copy.31 = bf16[4,10,64,2,64]{4,3,2,1,0:T(2,128)(2,1)} copy(bf16[4,10,64,2,64]{4,2,1,3,0:T(8,128)(2,1)S(1)} %bitcast.43) | data formatting | bytes 1310720 | tf_op jit(solution)/shard_map/transpose | solution.py:79
  196.6 0.0 copy-start.8
  196.6 2.8 %reshape.77 = bf16[40,64,128]{2,1,0:T(8,128)(2,1)S(1)} reshape(bf16[4,10,64,2,64]{4,3,2,1,0:T(2,128)(2,1)} %copy.31) | data formatting | bytes 1310720 | tf_op jit(solution)/shard_map/reshape | solution.py:80
  199.4 0.0 copy-done.8
  199.4 1.0 multiply_convert_fusion
  (5 shorter events, 0.1 us)
Async XLA Ops:
  6.6 2.0 copy-start.10
  8.6 0.9 copy-start.1
  8.6 1.0 copy-start.2
  9.3 72.4 %copy-start = (bf16[8,8,64,128]{3,1,2,0:T(8,128)(2,1)}, bf16[8,8,64,128]{3,1,2,0:T(8,128)(2,1)S(1)}, u32[]{:S(2)}) copy-start(bf16[8,8,64,128]{3,1,2,0:T(8,128)(2,1)S(1)} %copy.40) | copy-start | bytes 3145732
  81.7 2.2 %copy-start.3 = (bf16[192,12288]{1,0:T(8,128)(2,1)}, bf16[192,12288]{1,0:T(8,128)(2,1)S(1)}, u32[]{:S(2)}) copy-start(bf16[192,12288]{1,0:T(8,128)(2,1)S(1)} %get-tuple-element.20.refs_1_) | copy-start | bytes 14155780
  84.0 1.3 copy-start.5
  85.3 1.0 copy-start.6
  86.3 1.3 copy-start.4
  87.9 1.1 copy-start.7
  97.9 2.8 %copy-start.9 = (bf16[37,64,128]{2,1,0:T(8,128)(2,1)S(1)}, bf16[37,64,128]{2,1,0:T(8,128)(2,1)}, u32[]{:S(2)}) copy-start(bf16[37,64,128]{2,1,0:T(8,128)(2,1)} %param.11) | copy-start | bytes 1818628
  196.6 2.8 %copy-start.8 = (f32[5,8,64,128]{3,2,1,0:T(8,128)S(1)}, f32[5,8,64,128]{3,2,1,0:T(8,128)}, u32[]{:S(2)}) copy-start(f32[5,8,64,128]{3,2,1,0:T(8,128)} %copy-done.7) | copy-start | bytes 3932164

commit v2 on v1

--- a/solution.py
+++ b/solution.py
@@ -70,14 +70,26 @@
     each = -(-planes // rows)
     halves = lanes // edge
     padded = jnp.pad(tensor, ((0, each * rows - planes), (0, 0), (0, 0)))
-    turned = padded.reshape(rows, each, edge, halves, edge).transpose(0, 3, 1, 4, 2)
-    return turned.reshape(rows, halves, each, edge * edge // 128, 128)
+    turned = padded.reshape(rows, each, edge, lanes).transpose(0, 1, 3, 2)
+    fold, deep = 128 // edge, edge * edge // 128
+    pieces = []
+    for half in range(halves):
+        first = half * edge
+        parts = [
+            turned[:, :, first + u * deep : first + (u + 1) * deep] for u in range(fold)
+        ]
+        pieces.append(jnp.concatenate(parts, axis=3))
+    return jnp.stack(pieces, axis=1)
 
 
 def mirror_unpack(arrived, planes, edge):
     rows, halves, each = arrived.shape[:3]
-    turned = arrived.reshape(rows, halves, each, edge, edge).transpose(0, 2, 3, 1, 4)
-    return turned.reshape(rows * each, edge, halves * edge)[:planes]
+    fold = 128 // edge
+    sides = []
+    for half in range(halves):
+        parts = [arrived[:, half, :, :, u * edge : (u + 1) * edge] for u in range(fold)]
+        sides.append(jnp.concatenate(parts, axis=2))
+    return jnp.concatenate(sides, axis=3).reshape(rows * each, edge, halves * edge)[:planes]
 
 
 class Mirror:
@@ -236,10 +248,10 @@
 
     def weight_scratch(self, depth):
         return [
-            pltpu.VMEM((self.cols * depth, 256), jnp.float32),
-            pltpu.VMEM((self.cols, depth, 256), jnp.float32),
-            pltpu.VMEM((self.rows, depth, 256), jnp.float32),
-            pltpu.VMEM((self.cols, depth, 256), jnp.float32),
+            pltpu.VMEM((self.cols * depth, 128), jnp.float32),
+            pltpu.VMEM((self.cols, depth, 128), jnp.float32),
+            pltpu.VMEM((self.rows, depth, 128), jnp.float32),
+            pltpu.VMEM((self.cols, depth, 128), jnp.float32),
             dma(self.cols - 1),
             dma(self.cols - 1),
             dma(self.rows - 1),
@@ -395,15 +407,13 @@
 
 
 def weight_chunk(plan, wide, gradient, index):
-    return [
-        lax.dot_general(
-            gradient,
-            wide[:, plan.at(index, b * plan.margin)],
-            (((1,), (1,)), ((), ())),
-            preferred_element_type=jnp.float32,
-        )
-        for b in range(3)
-    ]
+    windows = [wide[:, plan.at(index, b * plan.margin)] for b in range(3)]
+    return lax.dot_general(
+        jnp.concatenate(windows, axis=0),
+        gradient,
+        (((1,), (1,)), ((), ())),
+        preferred_element_type=jnp.float32,
+    )
 
 
 def total_sums(plan, pair, over_row, over_col, row_out, row_in, col_out, col_in):
@@ -437,7 +447,6 @@
     clear(plan, wide_x, ends_x[2], ends_x[3])
     clear(plan, wide_h, ends_h[2], ends_h[3])
     meet(plan.rows, plan.cols)
-    mirror.hop_one()
     build_taps(k_first, w_first, False)
     build_taps(k_second, w_second, False)
 
@@ -449,6 +458,7 @@
     copies = halo_copies(plan, wide_x, *ends_x)
     halo_start(copies)
     halo_wait(copies)
+    mirror.hop_one()
     mend(plan, wide_x, ends_x[2], ends_x[3])
 
     def convolve(wide, weight):
@@ -480,8 +490,8 @@
     copies = halo_copies(plan, wide_h, *ends_h)
     halo_start(copies)
     halo_wait(copies)
+    mend(plan, wide_h, ends_h[2], ends_h[3])
     mirror.hop_three()
-    mend(plan, wide_h, ends_h[2], ends_h[3])
     average_2, inverse_2 = moments(convolve(wide_h, w_second), sums_second, inv_second)
 
     def tail(index, carry):
@@ -509,7 +519,9 @@
     late = WeightSum(plan.rows, plan.cols, depths[0], refs[47:57])
     early = WeightSum(plan.rows, plan.cols, depths[1], refs[57:67])
     mirror = Mirror(plan.rows, plan.cols, turned, landing, refs[67:75])
+    piled = refs[75]
     n, bins = plan.channels, sym.shape[0]
+    folded = 9 * n // 2
     zero = jnp.zeros((n, 1), jnp.float32)
     clear(plan, wide_2, ends_2[2], ends_2[3])
     clear(plan, wide_1, ends_1[2], ends_1[3])
@@ -519,7 +531,7 @@
     mirror.hop_one()
     build_taps(k_first, w_first, True)
     build_taps(k_second, w_second, True)
-    head_at = 3 * n
+    head_at = folded
 
     def start(index, carry):
         place = plan.at(index)
@@ -532,8 +544,8 @@
             sym_part, hidden[:, place], (((1,), (1,)), ((), ())),
             preferred_element_type=jnp.float32,
         )
-        early.mine[head_at : head_at + bins, 128:256] += jnp.broadcast_to(
-            jnp.sum(sym_part.astype(jnp.float32), axis=1, keepdims=True), (bins, 128)
+        early.mine[head_at : head_at + bins, n:] += jnp.broadcast_to(
+            jnp.sum(sym_part.astype(jnp.float32), axis=1, keepdims=True), (bins, 128 - n)
         )
         found = pair_of(part, part * n_second[:, place])
         return carry[0] + found[0], carry[1] + found[1]
@@ -560,20 +572,21 @@
     def weigh(wide, against, table):
         def body(index, carry):
             gradient = wide[n : 2 * n, plan.at(index, plan.margin)]
-            for b, part in enumerate(weight_chunk(plan, against, gradient, index)):
-                table.mine[b * n : (b + 1) * n, 0 : 3 * n] += part
+            piled[...] += weight_chunk(plan, against, gradient, index)
             return carry
 
+        piled[...] = jnp.zeros_like(piled)
         lax.fori_loop(0, plan.chunks, body, 0)
+        table.mine[0:folded, :] = jnp.concatenate([piled[0:folded], piled[folded:]], axis=1)
 
     copies = step_back(
         pair, sums_2, slope_grad, n_second, inv_second, wide_2, ends_2, mirror.hop_two
     )
     weigh(wide_2, wide_h, early)
     halo_wait(copies)
+    mend(plan, wide_2, ends_2[2], ends_2[3])
     mirror.hop_three()
     early.scatter()
-    mend(plan, wide_2, ends_2[2], ends_2[3])
 
     def through(index, carry):
         place = plan.at(index)
@@ -673,7 +686,7 @@
             *plan.mirror_scratch(turned),
         ],
         compiler_params=pltpu.CompilerParams(
-            collective_id=0, has_side_effects=True, vmem_limit_bytes=40 * 2**20
+            collective_id=0, has_side_effects=True, vmem_limit_bytes=32 * 2**20
         ),
         cost_estimate=pl.CostEstimate(
             flops=20 * flops, bytes_accessed=200 * 2**20, transcendentals=0
@@ -686,8 +699,9 @@
     sym = jnp.pad(grad_sym.reshape(bins, cells), ((0, padded - bins), (0, 0)))
     raw_logits = raw[:bins].reshape(bins, height, lanes)
     turned = mirror_pack(raw_logits.astype(jnp.bfloat16), rows)
-    depths = (plan.depth(3 * channels), plan.depth(3 * channels + padded))
-    sum_shapes = [jax.ShapeDtypeStruct((cols, depth, 256), jnp.float32) for depth in depths]
+    folded = 9 * channels // 2
+    depths = (plan.depth(folded), plan.depth(folded + padded))
+    sum_shapes = [jax.ShapeDtypeStruct((cols, depth, 128), jnp.float32) for depth in depths]
     grad_x, sum_first, sum_second, arrived = pl.pallas_call(
         functools.partial(backward_kernel, plan, cell_count, depths),
         out_shape=(short_shape, *sum_shapes, landing_shape),
@@ -707,9 +721,10 @@
             *plan.weight_scratch(depths[0]),
             *plan.weight_scratch(depths[1]),
             *plan.mirror_scratch(turned),
+            pltpu.VMEM((9 * channels, channels), jnp.float32),
         ],
         compiler_params=pltpu.CompilerParams(
-            collective_id=1, has_side_effects=True, vmem_limit_bytes=52 * 2**20
+            collective_id=1, has_side_effects=True, vmem_limit_bytes=42 * 2**20
         ),
         cost_estimate=pl.CostEstimate(
             flops=20 * flops, bytes_accessed=200 * 2**20, transcendentals=0
@@ -723,19 +738,20 @@
     inverse_len = 1.0 / length
 
     def kernel_grad(table):
-        part = table[: 3 * channels, : 3 * channels] * inverse_len
-        part = part.reshape(3, channels, 3, channels).transpose(2, 0, 1, 3)
+        part = table[:folded] * inverse_len
+        part = jnp.concatenate([part[:, :channels], part[:, channels : 2 * channels]], axis=0)
+        part = part.reshape(3, 3, channels, channels).transpose(1, 0, 3, 2)
         return part.reshape(9, channels, channels)
 
-    sum_first, sum_second = sum_first.reshape(-1, 256), sum_second.reshape(-1, 256)
-    head = sum_second[3 * channels : 3 * channels + bins] * inverse_len
+    sum_first, sum_second = sum_first.reshape(-1, 128), sum_second.reshape(-1, 128)
+    head = sum_second[folded : folded + bins] * inverse_len
     return (
         logits,
         grad_x.reshape(channels, height, lanes),
         kernel_grad(sum_first),
         kernel_grad(sum_second),
         head[:, :channels],
-        head[:, 128],
+        head[:, channels],
     )
 
 

time: 201 us -> 178 us (0.89)
  local copies, waits for them, and re-layouts: 40.4 us -> 26.2 us
  Pallas kernels: 158 us -> 147 us
    reshape x12 -> x2, local copies, waits for them, and re-layouts: 17.8 us -> 1.73 us  [kernel_grad(): part = part.reshape(3, 3, channels, channels).transpose(1, 0, 3, 2)]
    unnamed x29 -> x37, local copies, waits for them, and re-layouts: 12 us -> 19.3 us
    transpose x4 -> x0, local copies, waits for them, and re-layouts: 6.32 us -> none  [the longest x2 4.85 us: mirror_unpack(): arrived.reshape(rows, halves, each, edge, edge).transpose(0, 2, 3, 1, 4)]
    pallas_call x1, Pallas kernels: 72.1 us -> 66.5 us  [on_device(): pl.pallas_call(functools.partial(forward_kernel, plan, cell_count), out_s...]
    pallas_call x1, Pallas kernels: 85.7 us -> 80.7 us  [on_device(): pl.pallas_call(functools.partial(backward_kernel, plan, cell_count, depth...]
where the time goes in v2:
time: 178 us; the launch traced here: 177 us
  Pallas kernels  147 us (83%)
  local copies, waits for them, and re-layouts  26.2 us (15%)
  other arithmetic  2.93 us (2%)
    pallas_call x1, Pallas kernels, on_device(): pl.pallas_call(functools.partial(backward_kernel, plan, cell_count, depth...  80.7 us
    pallas_call x1, Pallas kernels, on_device(): pl.pallas_call(functools.partial(forward_kernel, plan, cell_count), out_s...  66.5 us
    unnamed x37, local copies, waits for them, and re-layouts  19.3 us

profile of v2, /device:TPU:0, one launch (start us, length us, event | category | flops | bytes accessed | tf_op | source)
XLA Modules:
  0.0 177.3 jit_solution(3744700467784762872)
XLA Ops:
  0.6 0.0 copy-start.12
  0.6 0.7 pad.20
  1.4 0.8 copy.26
  2.2 0.1 copy.47
  2.3 0.1 broadcast_in_dim.2.refs_4_
  2.4 1.9 %copy.52 = bf16[8,8,64,128]{3,1,2,0:T(8,128)(2,1)S(1)} copy(bf16[8,8,64,128]{3,2,1,0:T(8,128)(2,1)} %bitcast.79) | data formatting | bytes 2097152
  4.3 0.0 copy-done.12
  4.3 1.5 copy.40
  5.8 0.3 pad.21.clone
  6.2 0.3 fusion.1
  6.4 0.0 copy-start
  6.5 0.0 copy-start.1
  6.5 0.4 maximum_bitcast_fusion
  6.8 0.1 pad_maximum_fusion.refs_5_
  6.9 0.4 copy-done
  7.4 0.1 copy-done.1
  7.4 66.5 %shard_map.109 = (bf16[192,12288]{1,0:T(8,128)(2,1)S(1)}, bf16[192,12288]{1,0:T(8,128)(2,1)S(1)}, f32[64,8192]{1,0:T(8,128)S(1)}, f32[64,8192]{1,0:T(8,128)S(1)}...) custom-call(bf16[64,8192]{1,0:T(8,128)(2,1)S(1)} %bitcast.62, ...), custom_call_target="tpu_custom_call" | custom-call | flops 12079595520 | bytes 209715200 | tf_op jit(solution)/shard_map/pallas_call | solution.py:663
  74.0 0.0 copy-start.2
  74.0 2.1 %copy-done.2 = bf16[192,12288]{1,0:T(8,128)(2,1)} copy-done((bf16[192,12288]{1,0:T(8,128)(2,1)}, bf16[192,12288]{1,0:T(8,128)(2,1)S(1)}, u32[]{:S(2)}) %copy-start.2) | copy-done | bytes 4718616
  76.1 0.0 copy-start.3
  76.1 2.2 %copy-done.3 = bf16[192,12288]{1,0:T(8,128)(2,1)} copy-done((bf16[192,12288]{1,0:T(8,128)(2,1)}, bf16[192,12288]{1,0:T(8,128)(2,1)S(1)}, u32[]{:S(2)}) %copy-start.3) | copy-done | bytes 4718616
  78.3 0.0 copy-start.6
  78.3 1.4 copy-done.6
  79.7 1.0 copy-done.8
  80.7 0.1 slice.89
  80.8 1.2 copy-done.4
  82.0 0.2 copy.43
  82.2 0.0 copy-start.10
  82.3 0.2 slice_bitcast_fusion.7
  82.4 0.2 slice_bitcast_fusion.5
  82.6 0.4 maximum_maximum_fusion
  83.0 0.2 multiply_convert_fusion.1
  83.2 0.1 pad.48
  83.3 0.4 copy.44
  83.7 0.1 pad.22.refs_7_
  83.8 0.0 copy-done.10
  83.8 0.1 slice.154
  83.9 1.7 copy.41
  85.6 1.7 pad.23.clone
  87.3 0.0 copy-start.7
  87.3 0.3 fusion
  87.6 0.0 copy-start.9
  87.6 0.2 maximum_bitcast_fusion.2
  87.8 0.0 copy-start.5
  87.8 0.2 maximum_bitcast_fusion.3
  88.0 0.1 pad_maximum_fusion.1.refs_12_
  88.1 0.8 copy-done.7
  88.9 0.3 copy-done.9
  89.2 0.7 copy-done.5
  89.9 80.7 %shard_map.110 = (bf16[64,8192]{1,0:T(8,128)(2,1)S(1)}, f32[8,40,128]{2,1,0:T(8,128)S(1)}, f32[8,48,128]{2,1,0:T(8,128)S(1)}, bf16[4,2,10,32,128]{4,3,2,1,0:T(8,128)(2,1)S(1)}) custom-call(bf16[64,8192]{1,0:T(8,128)(2,1)S(1)} %bitcast.63, bf16[192,12288]{1,0:T(8,128)(2,1)} %copy-done.2, bf16[192,12288]{1,0:T(8,128)(2,1)} %copy-done.3, ...), custom_call_target="tpu_custom_call" | custom-call | flops 12079595520 | bytes 209715200 | tf_op jit(solution)/shard_map/pallas_call | solution.py:705
  170.6 1.3 copy.45
  171.9 0.0 copy-start.13
  171.9 0.7 slice_reduce_fusion
  172.6 0.1 fusion.2
  172.8 0.9 copy.39
  173.6 0.1 fusion.3
  173.7 0.0 copy-done.13
  173.8 0.9 copy.38
  174.6 0.2 slice_bitcast_fusion.6
  174.8 0.2 slice_bitcast_fusion.2
  175.0 0.0 copy-start.11
  175.0 0.4 maximum_maximum_fusion.1
  175.4 0.9 copy-done.11
  176.3 1.0 multiply_convert_fusion
  (9 shorter events, 0.1 us)
Async XLA Ops:
  0.6 3.7 %copy-start.12 = (bf16[37,64,128]{2,1,0:T(8,128)(2,1)S(1)}, bf16[37,64,128]{2,1,0:T(8,128)(2,1)}, u32[]{:S(2)}) copy-start(bf16[37,64,128]{2,1,0:T(8,128)(2,1)} %param.11) | copy-start | bytes 1818628
  6.4 0.9 copy-start
  6.5 1.0 copy-start.1
  74.0 2.1 %copy-start.2 = (bf16[192,12288]{1,0:T(8,128)(2,1)}, bf16[192,12288]{1,0:T(8,128)(2,1)S(1)}, u32[]{:S(2)}) copy-start(bf16[192,12288]{1,0:T(8,128)(2,1)S(1)} %get-tuple-element.20.refs_1_) | copy-start | bytes 14155780
  76.1 2.2 %copy-start.3 = (bf16[192,12288]{1,0:T(8,128)(2,1)}, bf16[192,12288]{1,0:T(8,128)(2,1)S(1)}, u32[]{:S(2)}) copy-start(bf16[192,12288]{1,0:T(8,128)(2,1)S(1)} %get-tuple-element.21.refs_2_) | copy-start | bytes 14155780
  78.3 1.4 copy-start.6
  79.7 1.0 copy-start.8
  80.7 1.3 copy-start.4
  82.2 1.5 copy-start.10
  87.3 1.6 copy-start.7
  87.6 1.6 copy-start.9
  87.8 2.1 %copy-start.5 = (f32[64,8192]{1,0:T(8,128)S(1)}, f32[64,8192]{1,0:T(8,128)}, u32[]{:S(2)}) copy-start(f32[64,8192]{1,0:T(8,128)} %copy-done.4) | copy-start | bytes 6291460
  171.9 1.8 %copy-start.13 = (f32[37,128]{1,0:T(8,128)}, f32[37,128]{1,0:T(8,128)S(1)}, u32[]{:S(2)}) copy-start(f32[37,128]{1,0:T(8,128)S(1)} %slice_multiply_fusion.2) | copy-start | bytes 56836
  175.0 1.3 copy-start.11

commit v3 on v2

--- a/solution.py
+++ b/solution.py
@@ -231,6 +231,9 @@
             dma(self.cols - 1),
         ]
 
+    def line(self, index, m, offset=0):
+        return pl.ds(pl.multiple_of(index * self.chunk + offset + m * self.lanes, 128), self.lanes)
+
     def mirror_scratch(self, packed):
         return [
             pltpu.VMEM(packed.shape, jnp.bfloat16),
@@ -274,24 +277,21 @@
     high[...] = jnp.zeros_like(high)
 
 
-def emit(plan, wide, last, first, index, values):
+def emit(plan, wide, last, first, index, make):
     n, lanes, step = plan.channels, plan.lanes, DILATION_STEP
-    place = plan.at(index, plan.margin)
     lane = lax.broadcasted_iota(jnp.int32, (n, lanes), 1)
-    wide[n : 2 * n, place] = values.astype(jnp.bfloat16)
-    later, sooner = [], []
     tail, lead = jnp.zeros((n, lanes), jnp.float32), jnp.zeros((n, lanes), jnp.float32)
     for m in range(plan.group):
-        line = values[:, m * lanes : (m + 1) * lanes]
+        line = make(plan.line(index, m))
+        place = plan.line(index, m, plan.margin)
         right = pltpu.roll(line, step, 1)
         left = pltpu.roll(line, lanes - step, 1)
-        later.append(right.astype(jnp.bfloat16))
-        sooner.append(left.astype(jnp.bfloat16))
+        wide[n : 2 * n, place] = line.astype(jnp.bfloat16)
+        wide[0:n, place] = right.astype(jnp.bfloat16)
+        wide[2 * n : 3 * n, place] = left.astype(jnp.bfloat16)
         mine = (lane >= m * step) & (lane < (m + 1) * step)
         tail = jnp.where(mine, pltpu.roll(right, m * step, 1) if m else right, tail)
         lead = jnp.where(mine, pltpu.roll(line, m * step, 1) if m else line, lead)
-    wide[0:n, place] = jnp.concatenate(later, axis=1)
-    wide[2 * n : 3 * n, place] = jnp.concatenate(sooner, axis=1)
     spot = plan.at(index, 0, lanes)
     last[:, spot] = tail.astype(jnp.bfloat16)
     first[:, spot] = lead.astype(jnp.bfloat16)
@@ -356,28 +356,25 @@
     lane = lax.broadcasted_iota(jnp.int32, (n, lanes), 1)
 
     def fill(index, fresh):
-        place = plan.at(index)
         spot = plan.at(index, 0, lanes)
         before = low[:, spot].astype(jnp.float32)
         after = high[:, spot].astype(jnp.float32)
-        middle = wide[n : 2 * n, place].astype(jnp.float32) if fresh else None
-        old_later = None if fresh else wide[0:n, place].astype(jnp.float32)
-        old_sooner = None if fresh else wide[2 * n : 3 * n, place].astype(jnp.float32)
-        later, sooner = [], []
         for m in range(plan.group):
-            line = slice(m * lanes, (m + 1) * lanes)
+            place = plan.line(index, m)
             if fresh:
-                right = pltpu.roll(middle[:, line], step, 1)
-                left = pltpu.roll(middle[:, line], lanes - step, 1)
+                middle = wide[n : 2 * n, place].astype(jnp.float32)
+                right = pltpu.roll(middle, step, 1)
+                left = pltpu.roll(middle, lanes - step, 1)
             else:
-                right, left = old_later[:, line], old_sooner[:, line]
+                right = wide[0:n, place].astype(jnp.float32)
+                left = wide[2 * n : 3 * n, place].astype(jnp.float32)
             enter = pltpu.roll(before, (lanes - m * step) % lanes, 1) if m else before
             back = (lanes - step - m * step) % lanes
             leave = pltpu.roll(after, back, 1) if back else after
-            later.append(jnp.where(lane < step, enter, right).astype(jnp.bfloat16))
-            sooner.append(jnp.where(lane >= lanes - step, leave, left).astype(jnp.bfloat16))
-        wide[0:n, place] = jnp.concatenate(later, axis=1)
-        wide[2 * n : 3 * n, place] = jnp.concatenate(sooner, axis=1)
+            wide[0:n, place] = jnp.where(lane < step, enter, right).astype(jnp.bfloat16)
+            wide[2 * n : 3 * n, place] = jnp.where(
+                lane >= lanes - step, leave, left
+            ).astype(jnp.bfloat16)
 
     side = plan.margin // plan.chunk
 
@@ -431,8 +428,8 @@
     return back[0:n, 0:1], back[0:n, 1:2]
 
 
-def pair_of(first, second):
-    return jnp.sum(first, axis=1, keepdims=True), jnp.sum(second, axis=1, keepdims=True)
+def reduced(pair):
+    return tuple(jnp.sum(part, axis=1, keepdims=True) for part in pair)
 
 
 def forward_kernel(plan, cell_count, *refs):
@@ -443,7 +440,7 @@
     sums_first, sums_second = refs[30:36], refs[36:42]
     mirror = Mirror(plan.rows, plan.cols, turned, landing, refs[42:50])
     n = plan.channels
-    zero = jnp.zeros((n, 1), jnp.float32)
+    zero = jnp.zeros((n, plan.lanes), jnp.float32)
     clear(plan, wide_x, ends_x[2], ends_x[3])
     clear(plan, wide_h, ends_h[2], ends_h[3])
     meet(plan.rows, plan.cols)
@@ -451,7 +448,9 @@
     build_taps(k_second, w_second, False)
 
     def load(index, carry):
-        emit(plan, wide_x, ends_x[0], ends_x[1], index, x[:, plan.at(index)].astype(jnp.float32))
+        emit(
+            plan, wide_x, ends_x[0], ends_x[1], index, lambda at: x[:, at].astype(jnp.float32)
+        )
         return carry
 
     lax.fori_loop(0, plan.chunks, load, 0)
@@ -465,10 +464,13 @@
         def body(index, carry):
             part = conv_chunk(plan, wide, weight, index)
             act[:, plan.at(index)] = part
-            found = pair_of(part, part * part)
-            return carry[0] + found[0], carry[1] + found[1]
-
-        return lax.fori_loop(0, plan.chunks, body, (zero, zero))
+            total, square = carry
+            for m in range(plan.group):
+                line = part[:, m * plan.lanes : (m + 1) * plan.lanes]
+                total, square = total + line, square + line * line
+            return total, square
+
+        return reduced(lax.fori_loop(0, plan.chunks, body, (zero, zero)))
 
     def moments(pair, scratch, kept):
         totals, squares = total_sums(plan, pair, *scratch)
@@ -481,9 +483,12 @@
     mirror.hop_two()
 
     def middle(index, carry):
-        normed = (act[:, plan.at(index)] - average) * inverse
-        n_first[:, plan.at(index)] = normed
-        emit(plan, wide_h, ends_h[0], ends_h[1], index, elu_apply(normed))
+        def make(at):
+            normed = (act[:, at] - average) * inverse
+            n_first[:, at] = normed
+            return elu_apply(normed)
+
+        emit(plan, wide_h, ends_h[0], ends_h[1], index, make)
         return carry
 
     lax.fori_loop(0, plan.chunks, middle, 0)
@@ -496,12 +501,14 @@
 
     def tail(index, carry):
         place = plan.at(index)
-        normed = (act[:, place] - average_2) * inverse_2
-        n_second[:, place] = normed
-        out = elu_apply(normed + x[:, place].astype(jnp.float32)).astype(jnp.bfloat16)
-        hidden[:, place] = out
+        for m in range(plan.group):
+            at = plan.line(index, m)
+            normed = (act[:, at] - average_2) * inverse_2
+            n_second[:, at] = normed
+            out = elu_apply(normed + x[:, at].astype(jnp.float32))
+            hidden[:, at] = out.astype(jnp.bfloat16)
         raw[:, place] = (
-            jnp.dot(w_head[...], out, preferred_element_type=jnp.float32) + bias[:, 0:1]
+            jnp.dot(w_head[...], hidden[:, place], preferred_element_type=jnp.float32) + bias[:, 0:1]
         )
         return carry
 
@@ -522,7 +529,7 @@
     piled = refs[75]
     n, bins = plan.channels, sym.shape[0]
     folded = 9 * n // 2
-    zero = jnp.zeros((n, 1), jnp.float32)
+    zero = jnp.zeros((n, plan.lanes), jnp.float32)
     clear(plan, wide_2, ends_2[2], ends_2[3])
     clear(plan, wide_1, ends_1[2], ends_1[3])
     late.mine[...] = jnp.zeros_like(late.mine)
@@ -536,10 +543,15 @@
     def start(index, carry):
         place = plan.at(index)
         sym_part = sym[:, place]
-        summed = n_second[:, place] + x[:, place].astype(jnp.float32)
         part = jnp.dot(w_head[...], sym_part, preferred_element_type=jnp.float32)
-        part = part * elu_slope(summed)
-        slope_grad[:, place] = part
+        total, cross = carry
+        for m in range(plan.group):
+            at = plan.line(index, m)
+            normed = n_second[:, at]
+            line = part[:, m * plan.lanes : (m + 1) * plan.lanes]
+            line = line * elu_slope(normed + x[:, at].astype(jnp.float32))
+            slope_grad[:, at] = line
+            total, cross = total + line, cross + line * normed
         early.mine[head_at : head_at + bins, 0:n] += lax.dot_general(
             sym_part, hidden[:, place], (((1,), (1,)), ((), ())),
             preferred_element_type=jnp.float32,
@@ -547,10 +559,9 @@
         early.mine[head_at : head_at + bins, n:] += jnp.broadcast_to(
             jnp.sum(sym_part.astype(jnp.float32), axis=1, keepdims=True), (bins, 128 - n)
         )
-        found = pair_of(part, part * n_second[:, place])
-        return carry[0] + found[0], carry[1] + found[1]
-
-    pair = lax.fori_loop(0, plan.chunks, start, (zero, zero))
+        return total, cross
+
+    pair = reduced(lax.fori_loop(0, plan.chunks, start, (zero, zero)))
 
     def step_back(pair, scratch, source, normed, inverse_ref, wide, ends, beside):
         first_sum, second_sum = total_sums(plan, pair, *scratch)
@@ -559,9 +570,10 @@
         inverse = inverse_ref[:, 0:1]
 
         def body(index, carry):
-            place = plan.at(index)
-            value = inverse * (source[:, place] - first_mean - normed[:, place] * second_mean)
-            emit(plan, wide, ends[0], ends[1], index, value)
+            def make(at):
+                return inverse * (source[:, at] - first_mean - normed[:, at] * second_mean)
+
+            emit(plan, wide, ends[0], ends[1], index, make)
             return carry
 
         lax.fori_loop(0, plan.chunks, body, 0)
@@ -589,14 +601,17 @@
     early.scatter()
 
     def through(index, carry):
-        place = plan.at(index)
-        normed = n_first[:, place]
-        part = conv_chunk(plan, wide_2, w_second, index) * elu_slope(normed)
-        inner_grad[:, place] = part
-        found = pair_of(part, part * normed)
-        return carry[0] + found[0], carry[1] + found[1]
-
-    pair = lax.fori_loop(0, plan.chunks, through, (zero, zero))
+        part = conv_chunk(plan, wide_2, w_second, index)
+        total, cross = carry
+        for m in range(plan.group):
+            at = plan.line(index, m)
+            normed = n_first[:, at]
+            line = part[:, m * plan.lanes : (m + 1) * plan.lanes] * elu_slope(normed)
+            inner_grad[:, at] = line
+            total, cross = total + line, cross + line * normed
+        return total, cross
+
+    pair = reduced(lax.fori_loop(0, plan.chunks, through, (zero, zero)))
     early.across()
     copies = step_back(
         pair, sums_1, inner_grad, n_first, inv_first, wide_1, ends_1, early.gather
@@ -686,7 +701,7 @@
             *plan.mirror_scratch(turned),
         ],
         compiler_params=pltpu.CompilerParams(
-            collective_id=0, has_side_effects=True, vmem_limit_bytes=32 * 2**20
+            collective_id=0, has_side_effects=True, vmem_limit_bytes=12 * 2**20
         ),
         cost_estimate=pl.CostEstimate(
             flops=20 * flops, bytes_accessed=200 * 2**20, transcendentals=0
@@ -724,7 +739,7 @@
             pltpu.VMEM((9 * channels, channels), jnp.float32),
         ],
         compiler_params=pltpu.CompilerParams(
-            collective_id=1, has_side_effects=True, vmem_limit_bytes=42 * 2**20
+            collective_id=1, has_side_effects=True, vmem_limit_bytes=26 * 2**20
         ),
         cost_estimate=pl.CostEstimate(
             flops=20 * flops, bytes_accessed=200 * 2**20, transcendentals=0

time: 178 us -> 184 us (1.034)
  local copies, waits for them, and re-layouts: 26.2 us -> 30.9 us
    unnamed x37 -> x41, local copies, waits for them, and re-layouts: 19.3 us -> 24 us
    pallas_call x1, Pallas kernels: 66.5 us -> 69.4 us  [on_device(): pl.pallas_call(functools.partial(forward_kernel, plan, cell_count), out_s...]
where the time goes in v3:
time: 184 us; the launch traced here: 183 us
  Pallas kernels  148 us (80%)
  local copies, waits for them, and re-layouts  30.9 us (17%)
  other arithmetic  2.93 us (2%)
    pallas_call x1, Pallas kernels, on_device(): pl.pallas_call(functools.partial(backward_kernel, plan, cell_count, depth...  78.9 us
    pallas_call x1, Pallas kernels, on_device(): pl.pallas_call(functools.partial(forward_kernel, plan, cell_count), out_s...  69.4 us
    unnamed x41, local copies, waits for them, and re-layouts  24 us

profile of v3, /device:TPU:0, one launch (start us, length us, event | category | flops | bytes accessed | tf_op | source)
XLA Modules:
  0.0 183.1 jit_solution(8991688588892597155)
XLA Ops:
  0.6 0.0 copy-start.14
  0.6 0.7 pad.20
  1.4 0.8 copy.26
  2.2 0.1 copy.47
  2.3 0.1 broadcast_in_dim.2.refs_4_
  2.4 1.9 %copy.52 = bf16[8,8,64,128]{3,1,2,0:T(8,128)(2,1)S(1)} copy(bf16[8,8,64,128]{3,2,1,0:T(8,128)(2,1)} %bitcast.79) | data formatting | bytes 2097152
  4.3 0.0 copy-done.14
  4.3 1.5 copy.40
  5.8 0.3 pad.21.clone
  6.2 0.3 fusion.1
  6.4 0.0 copy-start
  6.5 0.0 copy-start.1
  6.5 0.4 maximum_bitcast_fusion
  6.8 0.1 pad_maximum_fusion.refs_5_
  6.9 0.4 copy-done
  7.4 0.1 copy-done.1
  7.4 69.4 %shard_map.109 = (bf16[192,12288]{1,0:T(8,128)(2,1)S(1)}, bf16[192,12288]{1,0:T(8,128)(2,1)S(1)}, f32[64,8192]{1,0:T(8,128)S(1)}, f32[64,8192]{1,0:T(8,128)S(1)}...) custom-call(bf16[64,8192]{1,0:T(8,128)(2,1)S(1)} %bitcast.62, ...), custom_call_target="tpu_custom_call" | custom-call | flops 12079595520 | bytes 209715200 | tf_op jit(solution)/shard_map/pallas_call | solution.py:678
  76.8 0.0 copy-start.2
  76.9 2.1 %copy-done.2 = bf16[192,12288]{1,0:T(8,128)(2,1)} copy-done((bf16[192,12288]{1,0:T(8,128)(2,1)}, bf16[192,12288]{1,0:T(8,128)(2,1)S(1)}, u32[]{:S(2)}) %copy-start.2) | copy-done | bytes 4718616
  79.0 2.2 %copy-done.4 = bf16[192,12288]{1,0:T(8,128)(2,1)} copy-done((bf16[192,12288]{1,0:T(8,128)(2,1)}, bf16[192,12288]{1,0:T(8,128)(2,1)S(1)}, u32[]{:S(2)}) %copy-start.4) | copy-done | bytes 4718616
  81.2 1.4 copy-done.8
  82.6 1.0 copy-done.10
  83.6 0.1 slice.89
  83.7 1.2 copy-done.6
  84.9 0.2 copy.43
  85.1 0.0 copy-start.12
  85.2 0.2 slice_bitcast_fusion.7
  85.3 0.2 slice_bitcast_fusion.5
  85.5 0.4 maximum_maximum_fusion
  85.9 0.2 multiply_convert_fusion.1
  86.1 0.1 pad.48
  86.2 0.4 copy.44
  86.6 0.1 pad.22.refs_7_
  86.7 0.0 copy-done.12
  86.7 0.1 slice.154
  86.8 1.7 copy.41
  88.5 1.6 pad.23.clone
  90.1 0.0 copy-start.9
  90.1 0.3 fusion
  90.5 0.0 copy-start.11
  90.5 0.2 maximum_bitcast_fusion.2
  90.7 0.0 copy-start.7
  90.7 0.2 maximum_bitcast_fusion.3
  90.9 0.1 pad_maximum_fusion.1.refs_12_
  90.9 0.8 copy-done.9
  91.7 0.3 copy-done.11
  92.0 0.7 copy-done.7
  92.8 2.3 %copy-done.3 = bf16[192,12288]{1,0:T(8,128)(2,1)S(1)} copy-done((bf16[192,12288]{1,0:T(8,128)(2,1)S(1)}, bf16[192,12288]{1,0:T(8,128)(2,1)}, u32[]{:S(2)}) %copy-start.3) | copy-done | bytes 4718616
  95.1 2.3 %copy-done.5 = bf16[192,12288]{1,0:T(8,128)(2,1)S(1)} copy-done((bf16[192,12288]{1,0:T(8,128)(2,1)S(1)}, bf16[192,12288]{1,0:T(8,128)(2,1)}, u32[]{:S(2)}) %copy-start.5) | copy-done | bytes 4718616
  97.5 78.9 %shard_map.110 = (bf16[64,8192]{1,0:T(8,128)(2,1)S(1)}, f32[8,40,128]{2,1,0:T(8,128)S(1)}, f32[8,48,128]{2,1,0:T(8,128)S(1)}, bf16[4,2,10,32,128]{4,3,2,1,0:T(8,128)(2,1)S(1)}) custom-call(bf16[64,8192]{1,0:T(8,128)(2,1)S(1)} %bitcast.63, bf16[192,12288]{1,0:T(8,128)(2,1)S(1)} %copy-done.3, bf16[192,12288]{1,0:T(8,128)(2,1)S(1)} %copy-done.5, ...), custom_call_target="tpu_custom_call" | custom-call | flops 12079595520 | bytes 209715200 | tf_op jit(solution)/shard_map/pallas_call | solution.py:720
  176.3 1.3 copy.45
  177.6 0.0 copy-start.15
  177.6 0.7 slice_reduce_fusion
  178.3 0.1 fusion.2
  178.5 0.9 copy.39
  179.3 0.1 fusion.3
  179.4 0.0 copy-done.15
  179.5 0.9 copy.38
  180.4 0.2 slice_bitcast_fusion.6
  180.5 0.2 slice_bitcast_fusion.2
  180.7 0.0 copy-start.13
  180.7 0.4 maximum_maximum_fusion.1
  181.1 0.9 copy-done.13
  182.0 1.0 multiply_convert_fusion
  (13 shorter events, 0.1 us)
Async XLA Ops:
  0.6 3.7 %copy-start.14 = (bf16[37,64,128]{2,1,0:T(8,128)(2,1)S(1)}, bf16[37,64,128]{2,1,0:T(8,128)(2,1)}, u32[]{:S(2)}) copy-start(bf16[37,64,128]{2,1,0:T(8,128)(2,1)} %param.11) | copy-start | bytes 1818628
  6.4 0.9 copy-start
  6.5 1.0 copy-start.1
  76.8 2.1 %copy-start.2 = (bf16[192,12288]{1,0:T(8,128)(2,1)}, bf16[192,12288]{1,0:T(8,128)(2,1)S(1)}, u32[]{:S(2)}) copy-start(bf16[192,12288]{1,0:T(8,128)(2,1)S(1)} %get-tuple-element.20.refs_1_) | copy-start | bytes 14155780
  79.0 2.2 %copy-start.4 = (bf16[192,12288]{1,0:T(8,128)(2,1)}, bf16[192,12288]{1,0:T(8,128)(2,1)S(1)}, u32[]{:S(2)}) copy-start(bf16[192,12288]{1,0:T(8,128)(2,1)S(1)} %get-tuple-element.21.refs_2_) | copy-start | bytes 14155780
  81.2 1.5 copy-start.8
  82.6 1.0 copy-start.10
  83.6 1.3 copy-start.6
  85.1 1.5 copy-start.12
  90.1 1.6 copy-start.9
  90.5 1.6 copy-start.11
  90.7 2.1 %copy-start.7 = (f32[64,8192]{1,0:T(8,128)S(1)}, f32[64,8192]{1,0:T(8,128)}, u32[]{:S(2)}) copy-start(f32[64,8192]{1,0:T(8,128)} %copy-done.6) | copy-start | bytes 6291460
  92.8 2.3 %copy-start.3 = (bf16[192,12288]{1,0:T(8,128)(2,1)S(1)}, bf16[192,12288]{1,0:T(8,128)(2,1)}, u32[]{:S(2)}) copy-start(bf16[192,12288]{1,0:T(8,128)(2,1)} %copy-done.2) | copy-start | bytes 14155780
  95.1 2.3 %copy-start.5 = (bf16[192,12288]{1,0:T(8,128)(2,1)S(1)}, bf16[192,12288]{1,0:T(8,128)(2,1)}, u32[]{:S(2)}) copy-start(bf16[192,12288]{1,0:T(8,128)(2,1)} %copy-done.4) | copy-start | bytes 14155780
  177.6 1.8 copy-start.15
  180.7 1.3 copy-start.13

commit v4 on v2

--- a/solution.py
+++ b/solution.py
@@ -437,7 +437,8 @@
 
 def forward_kernel(plan, cell_count, *refs):
     x, k_first, k_second, w_head, bias, turned = refs[:6]
-    wide_x, wide_h, n_first, n_second, raw, hidden, inv_first, inv_second, landing = refs[6:15]
+    kept_x, kept_h, kept_n, n_second, raw, hidden, inv_first, inv_second, landing = refs[6:15]
+    wide_x, wide_h, n_first, keep_sem = refs[50:54]
     act, w_first, w_second = refs[15:18]
     ends_x, ends_h = refs[18:24], refs[24:30]
     sums_first, sums_second = refs[30:36], refs[36:42]
@@ -460,6 +461,8 @@
     halo_wait(copies)
     mirror.hop_one()
     mend(plan, wide_x, ends_x[2], ends_x[3])
+    keep_x = pltpu.make_async_copy(wide_x, kept_x, keep_sem.at[0])
+    keep_x.start()
 
     def convolve(wide, weight):
         def body(index, carry):
@@ -487,10 +490,14 @@
         return carry
 
     lax.fori_loop(0, plan.chunks, middle, 0)
+    keep_n = pltpu.make_async_copy(n_first, kept_n, keep_sem.at[1])
+    keep_n.start()
     copies = halo_copies(plan, wide_h, *ends_h)
     halo_start(copies)
     halo_wait(copies)
     mend(plan, wide_h, ends_h[2], ends_h[3])
+    keep_h = pltpu.make_async_copy(wide_h, kept_h, keep_sem.at[2])
+    keep_h.start()
     mirror.hop_three()
     average_2, inverse_2 = moments(convolve(wide_h, w_second), sums_second, inv_second)
 
@@ -506,11 +513,12 @@
         return carry
 
     lax.fori_loop(0, plan.chunks, tail, 0)
+    finish([keep_x, keep_n, keep_h])
     mirror.end()
 
 
 def backward_kernel(plan, cell_count, depths, *refs):
-    (x, wide_x, wide_h, n_first, n_second, inv_first, inv_second) = refs[:7]
+    (x, kept_x, kept_h, kept_n, n_second, inv_first, inv_second) = refs[:7]
     sym, hidden, k_first, k_second, w_head, turned = refs[7:13]
     grad_x, sum_first, sum_second, landing = refs[13:17]
     wide_2, wide_1, slope_grad, inner_grad, w_first, w_second = refs[17:23]
@@ -519,7 +527,12 @@
     late = WeightSum(plan.rows, plan.cols, depths[0], refs[47:57])
     early = WeightSum(plan.rows, plan.cols, depths[1], refs[57:67])
     mirror = Mirror(plan.rows, plan.cols, turned, landing, refs[67:75])
-    piled = refs[75]
+    piled, wide_x, wide_h, n_first, keep_sem = refs[75:80]
+    fetch_x = pltpu.make_async_copy(kept_x, wide_x, keep_sem.at[0])
+    fetch_n = pltpu.make_async_copy(kept_n, n_first, keep_sem.at[1])
+    fetch_h = pltpu.make_async_copy(kept_h, wide_h, keep_sem.at[2])
+    for fetch in (fetch_h, fetch_n, fetch_x):
+        fetch.start()
     n, bins = plan.channels, sym.shape[0]
     folded = 9 * n // 2
     zero = jnp.zeros((n, 1), jnp.float32)
@@ -582,11 +595,14 @@
     copies = step_back(
         pair, sums_2, slope_grad, n_second, inv_second, wide_2, ends_2, mirror.hop_two
     )
+    fetch_h.wait()
     weigh(wide_2, wide_h, early)
     halo_wait(copies)
     mend(plan, wide_2, ends_2[2], ends_2[3])
     mirror.hop_three()
     early.scatter()
+
+    fetch_n.wait()
 
     def through(index, carry):
         place = plan.at(index)
@@ -601,6 +617,7 @@
     copies = step_back(
         pair, sums_1, inner_grad, n_first, inv_first, wide_1, ends_1, early.gather
     )
+    fetch_x.wait()
     weigh(wide_1, wide_x, late)
     halo_wait(copies)
     late.scatter()
@@ -659,6 +676,13 @@
     flops = 2 * 9 * channels * channels * cells
     turned = mirror_pack(cotangent, rows)
     landing_shape = jax.ShapeDtypeStruct(turned.shape, jnp.bfloat16)
+    kept_scratch = [
+        pltpu.VMEM((3 * channels, width), jnp.bfloat16),
+        pltpu.VMEM((3 * channels, width), jnp.bfloat16),
+        pltpu.VMEM((channels, cells), jnp.float32),
+        dma(3),
+    ]
+    outside = [pl.BlockSpec(memory_space=pl.ANY)] * 3
     taps_scratch = pltpu.VMEM((3, channels, 3 * channels), jnp.bfloat16)
     wide_x, wide_h, n_first, n_second, raw, hidden, inv_first, inv_second, arrived = pl.pallas_call(
         functools.partial(forward_kernel, plan, cell_count),
@@ -674,7 +698,7 @@
             landing_shape,
         ),
         in_specs=vmem(6),
-        out_specs=tuple(vmem(9)),
+        out_specs=(*outside, *vmem(6)),
         scratch_shapes=[
             pltpu.VMEM((channels, cells), jnp.float32),
             taps_scratch,
@@ -684,6 +708,7 @@
             *plan.sum_scratch(),
             *plan.sum_scratch(),
             *plan.mirror_scratch(turned),
+            *kept_scratch,
         ],
         compiler_params=pltpu.CompilerParams(
             collective_id=0, has_side_effects=True, vmem_limit_bytes=32 * 2**20
@@ -705,7 +730,7 @@
     grad_x, sum_first, sum_second, arrived = pl.pallas_call(
         functools.partial(backward_kernel, plan, cell_count, depths),
         out_shape=(short_shape, *sum_shapes, landing_shape),
-        in_specs=vmem(13),
+        in_specs=[*vmem(1), *outside, *vmem(9)],
         out_specs=tuple(vmem(4)),
         scratch_shapes=[
             pltpu.VMEM(wide_shape.shape, jnp.bfloat16),
@@ -722,6 +747,7 @@
             *plan.weight_scratch(depths[1]),
             *plan.mirror_scratch(turned),
             pltpu.VMEM((9 * channels, channels), jnp.float32),
+            *kept_scratch,
         ],
         compiler_params=pltpu.CompilerParams(
             collective_id=1, has_side_effects=True, vmem_limit_bytes=42 * 2**20

time: 178 us -> 174 us (0.978)
  Pallas kernels: 147 us -> 144 us
    pallas_call x1, Pallas kernels: 80.7 us -> 77.1 us  [on_device(): pl.pallas_call(functools.partial(backward_kernel, plan, cell_count, depth...]
where the time goes in v4:
time: 174 us
  Pallas kernels  144 us (83%)
  local copies, waits for them, and re-layouts  26.2 us (15%)
  other arithmetic  2.93 us (2%)
    pallas_call x1, Pallas kernels, on_device(): pl.pallas_call(functools.partial(backward_kernel, plan, cell_count, depth...  77.1 us
    pallas_call x1, Pallas kernels, on_device(): pl.pallas_call(functools.partial(forward_kernel, plan, cell_count), out_s...  66.9 us
    unnamed x37, local copies, waits for them, and re-layouts  19.3 us

profile of v4, /device:TPU:0, one launch (start us, length us, event | category | flops | bytes accessed | tf_op | source)
XLA Modules:
  0.0 174.1 jit_solution(13362358032895488212)
XLA Ops:
  0.6 0.0 copy-start.12
  0.6 0.7 pad.20
  1.4 0.8 copy.26
  2.2 0.1 copy.47
  2.3 0.1 broadcast_in_dim.2.refs_4_
  2.4 1.9 %copy.52 = bf16[8,8,64,128]{3,1,2,0:T(8,128)(2,1)S(1)} copy(bf16[8,8,64,128]{3,2,1,0:T(8,128)(2,1)} %bitcast.79) | data formatting | bytes 2097152
  4.3 0.0 copy-done.12
  4.3 1.5 copy.40
  5.8 0.3 pad.21.clone
  6.2 0.3 fusion.1
  6.4 0.0 copy-start
  6.5 0.0 copy-start.1
  6.5 0.4 maximum_bitcast_fusion
  6.8 0.1 pad_maximum_fusion.refs_5_
  6.9 0.4 copy-done
  7.4 0.1 copy-done.1
  7.4 66.9 %shard_map.109 = (bf16[192,12288]{1,0:T(8,128)(2,1)S(1)}, bf16[192,12288]{1,0:T(8,128)(2,1)S(1)}, f32[64,8192]{1,0:T(8,128)S(1)}, f32[64,8192]{1,0:T(8,128)S(1)}...) custom-call(bf16[64,8192]{1,0:T(8,128)(2,1)S(1)} %bitcast.62, ...), custom_call_target="tpu_custom_call" | custom-call | flops 12079595520 | bytes 209715200 | tf_op jit(solution)/shard_map/pallas_call | solution.py:687
  74.3 0.0 copy-start.2
  74.4 2.1 %copy-done.2 = bf16[192,12288]{1,0:T(8,128)(2,1)} copy-done((bf16[192,12288]{1,0:T(8,128)(2,1)}, bf16[192,12288]{1,0:T(8,128)(2,1)S(1)}, u32[]{:S(2)}) %copy-start.2) | copy-done | bytes 4718616
  76.5 0.0 copy-start.3
  76.5 2.2 %copy-done.3 = bf16[192,12288]{1,0:T(8,128)(2,1)} copy-done((bf16[192,12288]{1,0:T(8,128)(2,1)}, bf16[192,12288]{1,0:T(8,128)(2,1)S(1)}, u32[]{:S(2)}) %copy-start.3) | copy-done | bytes 4718616
  78.7 0.0 copy-start.6
  78.7 1.4 copy-done.6
  80.1 1.0 copy-done.8
  81.1 0.1 slice.89
  81.2 1.2 copy-done.4
  82.4 0.2 copy.43
  82.6 0.0 copy-start.10
  82.6 0.2 slice_bitcast_fusion.7
  82.8 0.2 slice_bitcast_fusion.5
  83.0 0.4 maximum_maximum_fusion
  83.3 0.2 multiply_convert_fusion.1
  83.6 0.1 pad.48
  83.6 0.4 copy.44
  84.1 0.1 pad.22.refs_7_
  84.1 0.0 copy-done.10
  84.2 0.1 slice.154
  84.3 1.7 copy.41
  86.0 1.7 pad.23.clone
  87.6 0.0 copy-start.7
  87.7 0.3 fusion
  88.0 0.0 copy-start.9
  88.0 0.2 maximum_bitcast_fusion.2
  88.2 0.0 copy-start.5
  88.2 0.2 maximum_bitcast_fusion.3
  88.4 0.1 pad_maximum_fusion.1.refs_12_
  88.5 0.8 copy-done.7
  89.2 0.3 copy-done.9
  89.6 0.7 copy-done.5
  90.3 77.1 %shard_map.110 = (bf16[64,8192]{1,0:T(8,128)(2,1)S(1)}, f32[8,40,128]{2,1,0:T(8,128)S(1)}, f32[8,48,128]{2,1,0:T(8,128)S(1)}, bf16[4,2,10,32,128]{4,3,2,1,0:T(8,128)(2,1)S(1)}) custom-call(bf16[64,8192]{1,0:T(8,128)(2,1)S(1)} %bitcast.63, bf16[192,12288]{1,0:T(8,128)(2,1)} %copy-done.2, bf16[192,12288]{1,0:T(8,128)(2,1)} %copy-done.3, ...), custom_call_target="tpu_custom_call" | custom-call | flops 12079595520 | bytes 209715200 | tf_op jit(solution)/shard_map/pallas_call | solution.py:730
  167.4 1.3 copy.45
  168.7 0.0 copy-start.13
  168.7 0.7 slice_reduce_fusion
  169.4 0.1 fusion.2
  169.5 0.9 copy.39
  170.4 0.1 fusion.3
  170.5 0.0 copy-done.13
  170.6 0.9 copy.38
  171.4 0.2 slice_bitcast_fusion.6
  171.6 0.2 slice_bitcast_fusion.2
  171.8 0.0 copy-start.11
  171.8 0.4 maximum_maximum_fusion.1
  172.2 0.9 copy-done.11
  173.1 1.0 multiply_convert_fusion
  (9 shorter events, 0.1 us)
Async XLA Ops:
  0.6 3.7 %copy-start.12 = (bf16[37,64,128]{2,1,0:T(8,128)(2,1)S(1)}, bf16[37,64,128]{2,1,0:T(8,128)(2,1)}, u32[]{:S(2)}) copy-start(bf16[37,64,128]{2,1,0:T(8,128)(2,1)} %param.11) | copy-start | bytes 1818628
  6.4 0.9 copy-start
  6.5 1.0 copy-start.1
  74.3 2.1 %copy-start.2 = (bf16[192,12288]{1,0:T(8,128)(2,1)}, bf16[192,12288]{1,0:T(8,128)(2,1)S(1)}, u32[]{:S(2)}) copy-start(bf16[192,12288]{1,0:T(8,128)(2,1)S(1)} %get-tuple-element.20.refs_1_) | copy-start | bytes 14155780
  76.5 2.2 %copy-start.3 = (bf16[192,12288]{1,0:T(8,128)(2,1)}, bf16[192,12288]{1,0:T(8,128)(2,1)S(1)}, u32[]{:S(2)}) copy-start(bf16[192,12288]{1,0:T(8,128)(2,1)S(1)} %get-tuple-element.21.refs_2_) | copy-start | bytes 14155780
  78.7 1.4 copy-start.6
  80.1 1.0 copy-start.8
  81.1 1.3 copy-start.4
  82.6 1.5 copy-start.10
  87.6 1.6 copy-start.7
  88.0 1.6 copy-start.9
  88.2 2.1 %copy-start.5 = (f32[64,8192]{1,0:T(8,128)S(1)}, f32[64,8192]{1,0:T(8,128)}, u32[]{:S(2)}) copy-start(f32[64,8192]{1,0:T(8,128)} %copy-done.4) | copy-start | bytes 6291460
  168.7 1.8 %copy-start.13 = (f32[37,128]{1,0:T(8,128)}, f32[37,128]{1,0:T(8,128)S(1)}, u32[]{:S(2)}) copy-start(f32[37,128]{1,0:T(8,128)S(1)} %slice_multiply_fusion.2) | copy-start | bytes 56836
  171.8 1.3 copy-start.11
